TPU v7x, 256 devices: a whole 4x4x8 slice. The times are simulated.
256 devices in a mesh: harm: 4 (over z_hi, core), space: 16 (over x, y), samp: 4 (over z_lo).
Axes of the slice: x: 4, y: 4, z: 8 (z_hi: 2, z_lo: 4; z = z_hi * 4 + z_lo), core: 2. Of those that a mesh axis runs over, the one named last changes fastest.
Arguments:
- coeffs: bfloat16 [32, 32768], P(('harm', 'samp'), 'space'), may hold values from -1.5 to 1.5
- curl_tiles: bfloat16 [256, 4, 128, 384], P('space'), may hold values from -0.25 to 0.25
- pattern: int32 [256, 4], P('space'), may hold values from 0 to 17, as said below
- region_ids: int32 [256], P('space'), may hold values from 0 to 3
- material_law: float32 [3, 4], replicated, may hold values from 0.3 to 3
- source: float32 [32, 32768], P(('harm', 'samp'), 'space'), may hold values from -6 to 6
Outputs:
- residual: float32 [32, 32768], P(('harm', 'samp'), 'space')
Inputs may be any that keep to these rules, and one draw needn't show every extreme that they name: `pattern`: entries index a space shard's window of 18 edge tiles: 0 is the last tile of the previous shard, 17 the first of the next, cyclically over the sector; the first entry of every row is the element tile's own position in its shard plus one.
All inputs are finite; a program needn't handle non-finite values.
Results may differ from a plain program's by a relative error of at most 0.0015.
Values may be sent and summed in bfloat16 or wider, within the bound.
A program may use at most 64 MiB of HBM per device.

v0:
```python
import math

import jax
import jax.numpy as jnp
from jax import lax
from jax.sharding import PartitionSpec as P

SAMPLES = 64
PARTS_SIZE = 32


def padded(block, sides, width):
    for axis, dim in sides:
        count = lax.axis_size(axis)
        forward = [(i, i + 1) for i in range(count - 1)]
        forward.append((count - 1, 0))
        backward = [(target, source) for source, target in forward]
        low = lax.ppermute(
            lax.slice_in_dim(block, block.shape[dim] - width, None, axis=dim), axis, forward
        )
        high = lax.ppermute(lax.slice_in_dim(block, 0, width, axis=dim), axis, backward)
        block = jnp.concatenate([low, block, high], axis=dim)
    return block


def passed_along(array, axis, by):
    devices = lax.axis_size(axis)
    return lax.ppermute(array, axis, [(i, (i + by) % devices) for i in range(devices)])


def transform_table():
    sample_ids = jnp.arange(SAMPLES, dtype=jnp.int32)[:, None]
    part_ids = jnp.arange(PARTS_SIZE, dtype=jnp.int32)[None, :]
    orders = 2 * (part_ids // 2) + 1
    phase = (orders * sample_ids % SAMPLES).astype(jnp.float32) * (2.0 * math.pi / SAMPLES)
    return jnp.where(part_ids % 2 == 0, jnp.cos(phase), jnp.sin(phase))


def sample_order(group_size):
    samples_here = SAMPLES // group_size
    half_here = samples_here // 2
    slots = jnp.arange(SAMPLES, dtype=jnp.int32)
    owner = slots // samples_here
    within = slots % samples_here
    return owner * half_here + within % half_here + within // half_here * (SAMPLES // 2)


def apply_reluctivity(density, region_ids, material_law, tile_count, tile_width):
    samples_here = density.shape[0]
    shaped = density.reshape(samples_here, tile_count, 3, tile_width)
    magnitude = jnp.sum(shaped * shaped, axis=2)
    region_hits = (
        region_ids[:, None] == jnp.arange(material_law.shape[1], dtype=jnp.int32)[None, :]
    ).astype(jnp.float32)
    region_law = jnp.dot(
        region_hits,
        material_law.T,
        precision=lax.Precision.HIGHEST,
        preferred_element_type=jnp.float32,
    )
    base_value = region_law[:, 0][None, :, None]
    knee_value = region_law[:, 1][None, :, None]
    rise_value = region_law[:, 2][None, :, None]
    reluct = base_value + rise_value * magnitude / (magnitude + knee_value)
    return (reluct[:, :, None, :] * shaped).reshape(samples_here, tile_count * 3 * tile_width)


def window_totals(contrib, pattern, tile_count):
    placement_hits = (
        pattern[:, :, None] == jnp.arange(tile_count + 2, dtype=jnp.int32)[None, None, :]
    ).astype(jnp.float32)
    return jnp.einsum("pgki,gkw->pwi", contrib, placement_hits, precision=lax.Precision.HIGHEST)


def per_device(coeffs, curl_tiles, pattern, region_ids, material_law, source):
    parts_here = coeffs.shape[0]
    tile_count, links, tile_width, comp_width = curl_tiles.shape
    group_size = lax.axis_size(("harm", "samp"))
    rank = lax.axis_index(("harm", "samp"))
    samples_here = SAMPLES // group_size
    window = padded(coeffs, (("space", 1),), tile_width)
    transform = transform_table()
    ordered = jnp.take(transform, sample_order(group_size), axis=0)
    window_tiles = window.reshape(parts_here, tile_count + 2, tile_width)
    picked = jnp.take(window_tiles, pattern.reshape(-1), axis=1).reshape(
        parts_here, tile_count, links, tile_width
    )
    flux_rows = jnp.einsum("pgki,gkij->pgj", picked, curl_tiles, preferred_element_type=jnp.float32)
    flux_rows = flux_rows.reshape(parts_here, tile_count * comp_width)
    own_samples = lax.dynamic_slice_in_dim(ordered, rank * samples_here, samples_here, 0)
    own_parts = lax.dynamic_slice_in_dim(ordered, rank * parts_here, parts_here, 1)
    row_block = own_parts
    density = lax.psum_scatter(
        jnp.dot(
            row_block,
            flux_rows,
            precision=lax.Precision.HIGHEST,
            preferred_element_type=jnp.float32,
        ),
        ("harm", "samp"),
        scatter_dimension=0,
        tiled=True,
    )
    field = apply_reluctivity(density, region_ids, material_law, tile_count, tile_width)
    row_block = own_samples
    harm_field = lax.psum_scatter(
        2.0
        / SAMPLES
        * jnp.dot(
            row_block.T, field, precision=lax.Precision.HIGHEST, preferred_element_type=jnp.float32
        ),
        ("harm", "samp"),
        scatter_dimension=0,
        tiled=True,
    )
    field_half = harm_field.astype(jnp.bfloat16).reshape(parts_here, tile_count, comp_width)
    contrib = jnp.einsum(
        "pgj,gkij->pgki", field_half, curl_tiles, preferred_element_type=jnp.float32
    )
    window_sum = window_totals(contrib, pattern, tile_count)
    from_right = passed_along(window_sum[:, 0], "space", -1)
    from_left = passed_along(window_sum[:, tile_count + 1], "space", 1)
    owned_sum = window_sum[:, 1 : tile_count + 1]
    owned_sum = owned_sum.at[:, 0].add(from_left)
    owned_sum = owned_sum.at[:, tile_count - 1].add(from_right)
    return owned_sum.reshape(parts_here, tile_count * tile_width) - source


def solution(mesh):
    placed = (
        P(("harm", "samp"), "space"),
        P("space", None, None, None),
        P("space", None),
        P("space"),
        P(),
        P(("harm", "samp"), "space"),
    )
    return jax.shard_map(
        per_device,
        mesh=mesh,
        in_specs=placed,
        out_specs=P(("harm", "samp"), "space"),
        check_vma=False,
    )
```

profile of v0, /device:TPU:1, one launch (start us, length us, event | category | flops | bytes accessed | tf_op | source)
XLA Modules:
  0.0 227.3 jit_solution(14497443400574377748)
XLA Ops:
  6.5 0.0 copy-start
  6.5 0.0 all-reduce.5.cloned.1.call-start
  6.5 0.7 fusion.37
  7.2 2.1 collective-permute-start
  9.4 3.6 %collective-permute-start.1 = (bf16[2,128]{1,0:T(2,128)(2,1)S(1)}, bf16[2,128]{1,0:T(2,128)(2,1)S(1)}, u32[]{:S(2)}, u32[]{:S(2)}) collective-permute-start(bf16[2,128]{1,0:T(2,128)(2,1)S(1)} %get-tuple-element.33), channel_id=1, source_target_pairs={{4,0},{8,4},{12,8},{16,12},{20,16},{24,20},{28,24},{32,28},{36,32}... | collective-permute-start | bytes 1544 | tf_op jit(solution)/shard_map/ppermute | solution.py:21
  13.0 0.8 copy.20
  13.7 0.7 compare_and_fusion
  14.5 0.1 reshape.327
  14.6 0.1 sine_select_fusion
  14.8 0.6 gather_fusion
  15.4 0.1 broadcast_select_fusion.2
  15.4 0.1 copy.19
  15.5 0.0 collective-permute-done
  15.5 0.0 collective-permute-done.1
  15.6 0.7 maximum_bitcast_fusion
  16.3 0.6 gather_fusion.1
  16.9 0.0 copy-start.4
  16.9 0.0 copy-start.3
  16.9 3.8 %fusion.6 = f32[16,2,384,1]{2,1,3,0:T(2,128)S(1)} fusion(bf16[16,4,128,384]{3,2,1,0:T(8,128)(2,1)} %param.11, bf16[2,16,4,128]{3,0,2,1:T(2,128)(2,1)S(1)} %bitcast.56, pred[16,4]{1,0:T(8,128)(4,1)S(1)} %copy.19), kind=kOutput, calls=%fused_computation.17 | convolution fusion | flops 12599296 | bytes 6373440 | tf_op jit(solution)/shard_map/pgki,gkij->pgj/dot_general | solution.py:88
  20.7 0.0 copy-start.1
  20.7 0.0 copy-start.2
  20.7 2.6 %fusion.7 = f32[64,6144]{1,0:T(8,128)} fusion(f32[2,6144]{1,0:T(2,128)S(1)} %bitcast.55, f32[64,32]{1,0:T(8,128)S(1)} %broadcast_select_fusion.2, s32[]{:T(128)S(6)} %select_n.156), kind=kOutput, calls=%fused_computation.19 | convolution fusion | flops 9437184 | bytes 1630212 | tf_op jit(solution)/shard_map/dot_general | solution.py:94
  23.3 0.0 all-reduce.5.cloned.1.call-update
  23.4 0.0 copy-done.4
  23.4 0.6 dynamic-slice.16
  25.3 0.0 copy-done
  25.3 0.0 copy-done.3
  25.3 0.2 fusion.16
  25.5 113.1 %all-reduce.5.cloned.1.call-done = f32[64,6144]{1,0:T(8,128)} async-done(((f32[64,6144]{1,0:T(8,128)}), f32[64,6144]{1,0:T(8,128)}) %all-reduce.5.cloned.1.call-update) | async-done | bytes 1572880
  138.6 0.9 dynamic-slice_multiply_fusion
  139.6 0.1 mul.126
  139.7 0.1 reduce_sum.9
  139.7 0.1 divide_add_fusion
  139.9 0.1 mul.129
  139.9 1.8 convolution_multiply_fusion
  141.7 67.4 %all-reduce.6 = bf16[32,6144]{1,0:T(8,128)(2,1)S(1)} all-reduce(f32[32,6144]{1,0:T(8,128)S(1)} %convolution_multiply_fusion), channel_id=3, replica_groups=mesh['harm'=4,'space'=16,'samp'=4] {'harm','samp'}, use_global_device_ids=true, to_apply=%region_2.3.clone | all-reduce | flops 196608 | bytes 1179648
  209.2 4.5 %convolution_bitcast_fusion = f32[2,16,4,128]{3,0,2,1:T(2,128)S(1)} fusion(bf16[2,16,384,1]{2,0,3,1:T(2,128)(2,1)S(1)} %bitcast.57, bf16[16,4,128,384]{3,2,1,0:T(8,128)(2,1)} %param.11), kind=kOutput, calls=%fused_computation.3 | convolution fusion | flops 12582912 | bytes 6381568 | tf_op jit(solution)/shard_map/pgj,gkij->pgki/dot_general | solution.py:117
  213.7 0.0 copy-done.1
  213.7 0.3 convolution_bitcast_fusion.1
  214.0 1.1 collective-permute-start.2
  215.1 3.8 %collective-permute-start.3 = (f32[2,128]{1,0:T(2,128)S(1)}, f32[2,128]{1,0:T(2,128)S(1)}, u32[]{:S(2)}, u32[]{:S(2)}) collective-permute-start(f32[2,128]{1,0:T(2,128)S(1)} %bitcast.59), channel_id=1, source_target_pairs={{0,60},{4,0},{8,4},{12,8},{16,12},{20,16},{24,20},{28,24},{32,28},... | collective-permute-start | bytes 3080 | tf_op jit(solution)/shard_map/ppermute | solution.py:28
  218.9 0.9 collective-permute-done.2
  219.8 0.0 collective-permute-done.3
  219.8 0.0 copy-done.2
  219.8 0.6 bitcast_subtract_fusion
  (15 shorter events, 0.2 us)
Async XLA Ops:
  6.5 18.7 %copy-start = (f32[3,4]{1,0:T(4,128)S(1)}, f32[3,4]{1,0:T(4,128)}, u32[]{:S(2)}) copy-start(f32[3,4]{1,0:T(4,128)} %param.14) | copy-start | bytes 148
  6.5 132.1 %all-reduce.5.cloned.1.call-start = ((), (), s32[]{:S(2)}) async-start(), calls=%async_computation | async-start | bytes 3145728
  7.2 8.3 %collective-permute-start = (bf16[2,128]{1,0:T(2,128)(2,1)S(1)}, bf16[2,128]{1,0:T(2,128)(2,1)S(1)}, u32[]{:S(2)}, u32[]{:S(2)}) collective-permute-start(bf16[2,128]{1,0:T(2,128)(2,1)S(1)} %get-tuple-element.32), channel_id=1, source_target_pairs={{0,4},{4,8},{8,12},{12,16},{16,20},{20,24},{24,28},{28,32},{32,36}... | collective-permute-start | bytes 1544 | tf_op jit(solution)/shard_map/ppermute | solution.py:18
  9.4 6.2 %collective-permute-start.1 = (bf16[2,128]{1,0:T(2,128)(2,1)S(1)}, bf16[2,128]{1,0:T(2,128)(2,1)S(1)}, u32[]{:S(2)}, u32[]{:S(2)}) collective-permute-start(bf16[2,128]{1,0:T(2,128)(2,1)S(1)} %get-tuple-element.33), channel_id=1, source_target_pairs={{4,0},{8,4},{12,8},{16,12},{20,16},{24,20},{28,24},{32,28},{36,32}... | collective-permute-start | bytes 1544 | tf_op jit(solution)/shard_map/ppermute | solution.py:21
  16.9 6.5 %copy-start.4 = (u32[256]{0:T(256)S(1)}, u32[256]{0:T(256)}, u32[]{:S(2)}) copy-start(u32[256]{0:T(256)} %constant.197) | copy-start | bytes 3076
  16.9 8.3 %copy-start.3 = (s32[16]{0:T(128)S(1)}, s32[16]{0:T(128)}, u32[]{:S(2)}) copy-start(s32[16]{0:T(128)} %param.13) | copy-start | bytes 196
  20.7 192.9 %copy-start.1 = (s32[16,4]{0,1:T(4,128)S(1)}, s32[16,4]{0,1:T(4,128)}, u32[]{:S(2)}) copy-start(s32[16,4]{0,1:T(4,128)} %param.12) | copy-start | bytes 772
  20.7 199.1 %copy-start.2 = (f32[2,2048]{1,0:T(2,128)S(1)}, f32[2,2048]{1,0:T(2,128)}, u32[]{:S(2)}) copy-start(f32[2,2048]{1,0:T(2,128)} %param.15) | copy-start | bytes 49156
  214.0 5.8 %collective-permute-start.2 = (f32[2,128]{1,0:T(2,128)S(1)}, f32[2,128]{1,0:T(2,128)S(1)}, u32[]{:S(2)}, u32[]{:S(2)}) collective-permute-start(f32[2,128]{1,0:T(2,128)S(1)} %bitcast.60), channel_id=1, source_target_pairs={{0,4},{4,8},{8,12},{12,16},{16,20},{20,24},{24,28},{28,32},{32,36}... | collective-permute-start | bytes 3080 | tf_op jit(solution)/shard_map/ppermute | solution.py:28
  215.1 4.7 %collective-permute-start.3 = (f32[2,128]{1,0:T(2,128)S(1)}, f32[2,128]{1,0:T(2,128)S(1)}, u32[]{:S(2)}, u32[]{:S(2)}) collective-permute-start(f32[2,128]{1,0:T(2,128)S(1)} %bitcast.59), channel_id=1, source_target_pairs={{0,60},{4,0},{8,4},{12,8},{16,12},{20,16},{24,20},{28,24},{32,28},... | collective-permute-start | bytes 3080 | tf_op jit(solution)/shard_map/ppermute | solution.py:28
Sparse Core Ops, SparseCore 0:
  23.5 115.0 all-reduce.4
where the time goes:
time: 228 us; the launch traced here: 227 us
  waiting for transfers between devices  114 us (50%)
  blocking collectives  67.4 us (30%)
  between operations  14.9 us (7%)
  matrix products  13.2 us (6%)
  starting transfers between devices  10.7 us (5%)
  local copies, waits for them, and re-layouts  3.74 us (2%)
  other arithmetic  3.42 us (2%)
    unnamed x2, waiting for transfers between devices  113 us
    unnamed x1, blocking collectives  67.4 us
    ppermute x2, starting transfers between devices, passed_along(): lax.ppermute(array, axis, [(i, (i + by) % devices) for i in range(devices)])  4.94 us
  transfers between devices with their start and end apart: 5, of which 2 were waited for; matrix products, arithmetic and copies ran while one was open for 1% of the time, Pallas kernels for 0%

commit v1 on v0

v1 whole, which is shorter than its diff:
```python
import math

import jax
import jax.numpy as jnp
import ml_dtypes
import numpy as np
from jax import lax
from jax.experimental import pallas as pl
from jax.experimental.pallas import tpu as pltpu
from jax.sharding import PartitionSpec as P

SAMPLES = 64
HALF = SAMPLES // 2
PARTS = 32
GROUP = 16
SPACE = 16
TILES = 16
LINKS = 4
TILE = 128
COMP = 3 * TILE
MESH = pl.DeviceIdType.MESH
F32, BF16 = jnp.float32, jnp.bfloat16


def two_pieces(table):
    high = table.astype(ml_dtypes.bfloat16)
    low = (table - high.astype(np.float64)).astype(ml_dtypes.bfloat16)
    return high, low


def tables():
    t = np.arange(HALF)[:, None]
    q = np.arange(PARTS)[None, :]
    phase = ((2 * (q // 2) + 1) * t % SAMPLES) * (2.0 * math.pi / SAMPLES)
    transform = np.where(q % 2 == 0, np.cos(phase), np.sin(phase))
    main = np.zeros((LINKS, HALF, GROUP, LINKS, 2))
    for k in range(LINKS):
        main[k, :, :, k, :] = transform.reshape(HALF, GROUP, 2)
    forward = np.concatenate(
        [
            main.reshape(LINKS * HALF, GROUP * LINKS * 2),
            np.tile(transform, (LINKS, 2)),
            np.zeros((LINKS * HALF, 64)),
        ],
        axis=1,
    )
    back = (4.0 / SAMPLES) * transform.reshape(HALF, GROUP, 2).transpose(2, 1, 0).reshape(PARTS, HALF)
    back_high, back_low = two_pieces(back)
    back_row = np.zeros((PARTS, 256), ml_dtypes.bfloat16)
    back_row[:, : 3 * HALF] = np.concatenate([back_high, back_low, back_high], axis=1)
    return np.concatenate([*two_pieces(forward), back_row], axis=0)


def split(value):
    high = value.astype(BF16)
    return high, (value - high.astype(F32)).astype(BF16)


def kernel(
    coef_hbm, curl_hbm, pat_hbm, reg_hbm, law_hbm, tab_hbm, out_ref,
    coef, curl, pat, reg, law, tab, picks, got, low_got, high_got, sums,
    flow, flow_got, edge_flow, low_flow, high_flow, local_sem, send_sem, recv_sem,
):
    harm, space, samp = lax.axis_index("harm"), lax.axis_index("space"), lax.axis_index("samp")
    rank = harm * 4 + samp

    def at(group, other):
        return (other // 4, group, lax.rem(other, 4))

    near = [lax.rem(rank + d, GROUP) for d in range(1, GROUP)]
    everyone = [lax.rem(rank + d, GROUP) for d in range(GROUP)]
    after, before = lax.rem(space + 1, SPACE), lax.rem(space + SPACE - 1, SPACE)

    loads = [
        pltpu.make_async_copy(coef_hbm, coef, local_sem.at[0]),
        pltpu.make_async_copy(pat_hbm, pat, local_sem.at[1]),
        pltpu.make_async_copy(reg_hbm, reg, local_sem.at[2]),
        pltpu.make_async_copy(law_hbm, law, local_sem.at[3]),
        pltpu.make_async_copy(tab_hbm, tab, local_sem.at[4]),
        pltpu.make_async_copy(curl_hbm.at[rank], curl, local_sem.at[5]),
    ]
    for load in loads:
        load.start()
    barrier = pltpu.get_barrier_semaphore()
    for other in near:
        pl.semaphore_signal(barrier, inc=1, device_id=at(space, other), device_id_type=MESH)
    for other in everyone:
        for group in (after, before):
            pl.semaphore_signal(barrier, inc=1, device_id=at(group, other), device_id_type=MESH)

    loads[0].wait()
    loads[1].wait()
    rows = jnp.concatenate(
        [jnp.broadcast_to(pat[e : e + 1, :], (2 * LINKS, LINKS)) for e in range(TILES)], axis=0
    )
    row = lax.broadcasted_iota(jnp.int32, (TILES * LINKS * 2, LINKS), 0)
    col = lax.broadcasted_iota(jnp.int32, (TILES * LINKS * 2, LINKS), 1)
    spot = jnp.sum(jnp.where(row // 2 % LINKS == col, rows, 0), axis=1, keepdims=True)
    row = lax.broadcasted_iota(jnp.int32, (TILES * LINKS * 2, TILES * 2), 0)
    col = lax.broadcasted_iota(jnp.int32, (TILES * LINKS * 2, TILES * 2), 1)
    hits = jnp.where((spot == col // 2 + 1) & (row % 2 == col % 2), 1.0, 0.0)
    own = coef[...].astype(F32)
    own = jnp.concatenate([own[:, w * TILE : (w + 1) * TILE] for w in range(TILES)], axis=0)
    picked = jnp.dot(hits.astype(BF16), own.astype(BF16), preferred_element_type=F32)
    picks[...] = picked.reshape(TILES, 2 * LINKS, TILE).astype(BF16)
    for e in range(TILES):
        pass
    spread = hits.T.astype(BF16)
    spread = jnp.concatenate([spread, spread], axis=1)

    own_row = lax.broadcasted_iota(jnp.int32, (TILES, LINKS), 0) == rank
    links = jnp.sum(jnp.where(own_row, pat[...], 0), axis=0, keepdims=True)
    loads[2].wait()
    loads[3].wait()
    region = reg[...].reshape(1, TILES)
    lane = lax.broadcasted_iota(jnp.int32, (1, TILES), 1)
    region = jnp.sum(jnp.where(lane == rank, region, 0), axis=1, keepdims=True)
    lane = lax.broadcasted_iota(jnp.int32, (3, 4), 1)
    own_law = jnp.sum(jnp.where(lane == region, law[...], 0.0), axis=1, keepdims=True)
    base, knee, rise = own_law[0:1], own_law[1:2], own_law[2:3]
    loads[4].wait()
    lane = lax.broadcasted_iota(jnp.int32, (1, 2 * PARTS), 1)
    halo_table = []
    for k in range(LINKS):
        link = links[:, k : k + 1]
        mask = jnp.where(link == jnp.where(lane < PARTS, 0, TILES + 1), 1.0, 0.0)
        for piece in range(2):
            at_row = (piece * LINKS + k) * HALF
            halo_table.append(
                (piece, k, tab[at_row : at_row + HALF, TILE : TILE + 2 * PARTS].astype(F32) * mask)
            )
    halo_table = jnp.concatenate([v for _, _, v in sorted(halo_table, key=lambda v: v[:2])], axis=0)
    table = jnp.concatenate([tab[0:256, 0:TILE], halo_table.astype(BF16)], axis=1)
    back = tab[256:288, 0 : 3 * HALF]
    loads[5].wait()

    pl.semaphore_wait(barrier, GROUP - 1 + 2 * GROUP)

    for other in near:
        pltpu.make_async_remote_copy(
            src_ref=picks.at[other], dst_ref=got.at[rank], send_sem=send_sem.at[0],
            recv_sem=recv_sem.at[0], device_id=at(space, other), device_id_type=MESH,
        ).start()
    first, last = coef.at[:, pl.ds(0, TILE)], coef.at[:, pl.ds((TILES - 1) * TILE, TILE)]
    for other in everyone:
        pltpu.make_async_remote_copy(
            src_ref=last, dst_ref=low_got.at[rank], send_sem=send_sem.at[1],
            recv_sem=recv_sem.at[1], device_id=at(after, other), device_id_type=MESH,
        ).start()
        pltpu.make_async_remote_copy(
            src_ref=first, dst_ref=high_got.at[rank], send_sem=send_sem.at[2],
            recv_sem=recv_sem.at[2], device_id=at(before, other), device_id_type=MESH,
        ).start()
    got[rank] = picks[rank]

    def total(src, dst, i):
        return pltpu.make_async_remote_copy(
            src_ref=src, dst_ref=dst, send_sem=send_sem.at[i], recv_sem=recv_sem.at[i],
            device_id=at(space, near[0]), device_id_type=MESH,
        )

    done = [
        total(picks.at[pl.ds(0, GROUP - 1)], got.at[pl.ds(0, GROUP - 1)], 0),
        total(low_got, low_got, 1),
        total(high_got, high_got, 2),
    ]
    for d in done:
        d.wait_recv()

    halo = [ref[...].astype(F32).reshape(PARTS, TILE).astype(BF16) for ref in (low_got, high_got)]
    window = jnp.concatenate([got[...].reshape(TILES * LINKS * 2, TILE), *halo], axis=0)
    waves = jnp.dot(table, window, preferred_element_type=F32)
    waves = waves[: LINKS * HALF] + waves[LINKS * HALF :]
    waves = jnp.concatenate([waves[k * HALF : (k + 1) * HALF] for k in range(LINKS)], axis=1)
    blocks = curl[...].reshape(LINKS * TILE, COMP)
    density = jnp.dot(
        jnp.concatenate(split(waves), axis=0), blocks, preferred_element_type=F32
    )
    density = density[:HALF] + density[HALF:]
    comps = [density[:, c * TILE : (c + 1) * TILE] for c in range(3)]
    square = comps[0] * comps[0] + comps[1] * comps[1] + comps[2] * comps[2]
    reluct = base + rise * square / (square + knee)
    field = jnp.concatenate([reluct * c for c in comps], axis=1)
    high, low = split(field)
    harmonic = jnp.dot(back, jnp.concatenate([high, high, low], axis=0), preferred_element_type=F32)
    contrib = lax.dot_general(
        harmonic.astype(BF16), blocks, (((1,), (1,)), ((), ())), preferred_element_type=F32
    )
    for k in range(LINKS):
        for p in range(2):
            flow[pl.ds(2 * k + p, GROUP, stride=2 * LINKS), :] = contrib[
                p * GROUP : (p + 1) * GROUP, k * TILE : (k + 1) * TILE
            ]
    for side, spot in enumerate((0, TILES + 1)):
        edge = jnp.zeros((PARTS, TILE), F32)
        for k in range(LINKS):
            edge = edge + jnp.where(
                links[:, k : k + 1] == spot, contrib[:, k * TILE : (k + 1) * TILE], 0.0
            )
        for p in range(2):
            edge_flow[side, :, p, :] = edge[p * GROUP : (p + 1) * GROUP]

    def block(ref, which):
        return ref.at[pl.ds(pl.multiple_of(which * 8, 8), 8)]

    for other in everyone:
        pltpu.make_async_remote_copy(
            src_ref=edge_flow.at[0, other], dst_ref=high_flow.at[rank], send_sem=send_sem.at[3],
            recv_sem=recv_sem.at[3], device_id=at(before, other), device_id_type=MESH,
        ).start()
        pltpu.make_async_remote_copy(
            src_ref=edge_flow.at[1, other], dst_ref=low_flow.at[rank], send_sem=send_sem.at[4],
            recv_sem=recv_sem.at[4], device_id=at(after, other), device_id_type=MESH,
        ).start()
    for other in near:
        pltpu.make_async_remote_copy(
            src_ref=block(flow, other), dst_ref=block(flow_got, rank), send_sem=send_sem.at[5],
            recv_sem=recv_sem.at[5], device_id=at(space, other), device_id_type=MESH,
        ).start()
    mine = pl.ds(pl.multiple_of(rank * 8, 8), 8)
    flow_got[mine, :] = flow[mine, :]

    done += [
        total(edge_flow.at[0], high_flow, 3),
        total(edge_flow.at[1], low_flow, 4),
        total(flow.at[pl.ds(0, 8 * (GROUP - 1))], flow_got.at[pl.ds(0, 8 * (GROUP - 1))], 5),
    ]
    for d in done[3:]:
        d.wait_recv()
    owned = jnp.dot(
        spread, jnp.concatenate(split(flow_got[...]), axis=0), preferred_element_type=F32
    )
    low_sum, high_sum = low_flow[0], high_flow[0]
    for e in range(1, TILES):
        low_sum, high_sum = low_sum + low_flow[e], high_sum + high_flow[e]
    for w in range(TILES):
        piece = owned[2 * w : 2 * w + 2]
        if w == 0:
            piece = piece + low_sum
        if w == TILES - 1:
            piece = piece + high_sum
        out_ref[:, w * TILE : (w + 1) * TILE] = piece
    for d in done:
        d.wait_send()


def per_device(coeffs, curl_tiles, pattern, region_ids, material_law, source):
    anywhere = pl.BlockSpec(memory_space=pltpu.HBM)
    total = pl.pallas_call(
        kernel,
        out_shape=jax.ShapeDtypeStruct(source.shape, F32),
        in_specs=[anywhere] * 6,
        out_specs=pl.BlockSpec(memory_space=pltpu.VMEM),
        scratch_shapes=[
            pltpu.VMEM((2, TILES * TILE), BF16),
            pltpu.VMEM((LINKS, TILE, COMP), BF16),
            pltpu.VMEM((TILES, LINKS), jnp.int32),
            pltpu.VMEM((TILES,), jnp.int32),
            pltpu.VMEM((3, 4), F32),
            pltpu.VMEM((288, 256), BF16),
            pltpu.VMEM((TILES, 2 * LINKS, TILE), BF16),
            pltpu.VMEM((GROUP, 2 * LINKS, TILE), BF16),
            pltpu.VMEM((GROUP, 2, TILE), BF16),
            pltpu.VMEM((GROUP, 2, TILE), BF16),
            pltpu.VMEM((8, TILE), F32),
            pltpu.VMEM((GROUP * 8, TILE), F32),
            pltpu.VMEM((GROUP * 8, TILE), F32),
            pltpu.VMEM((2, GROUP, 2, TILE), F32),
            pltpu.VMEM((GROUP, 2, TILE), F32),
            pltpu.VMEM((GROUP, 2, TILE), F32),
            pltpu.SemaphoreType.DMA((6,)),
            pltpu.SemaphoreType.DMA((6,)),
            pltpu.SemaphoreType.DMA((6,)),
        ],
        compiler_params=pltpu.CompilerParams(collective_id=0, has_side_effects=True),
        name="residual",
    )(coeffs, curl_tiles, pattern, region_ids, material_law, jnp.asarray(tables()))
    return total - source


def solution(mesh):
    placed = (
        P(("harm", "samp"), "space"),
        P("space", None, None, None),
        P("space", None),
        P("space"),
        P(),
        P(("harm", "samp"), "space"),
    )
    return jax.shard_map(
        per_device,
        mesh=mesh,
        in_specs=placed,
        out_specs=P(("harm", "samp"), "space"),
        check_vma=False,
    )
```

time: 228 us -> 32.2 us (0.14)
  waiting for transfers between devices: 114 us -> 0 us
  blocking collectives: 67.4 us -> 0 us
  Pallas kernels: 0 us -> 29.2 us
  between operations: 14.9 us -> 0.02 us
  matrix products: 13.2 us -> 0 us
  starting transfers between devices: 10.7 us -> 0 us
  local copies, waits for them, and re-layouts: 3.74 us -> 1.37 us
    unnamed x2 -> x0, waiting for transfers between devices: 113 us -> none
    unnamed x1 -> x0, blocking collectives: 67.4 us -> none
    pallas_call x0 -> x1, Pallas kernels: none -> 29.2 us  [per_device(): pl.pallas_call(kernel, out_shape=jax.ShapeDtypeStruct(source.shape, F32),...]
    dot_general x6 -> x0, matrix products: 13.2 us -> none  [the longest x1 4.5 us: per_device(): jnp.einsum('pgj,gkij->pgki', field_half, curl_tiles, preferred_element_ty...]
    ppermute x4 -> x0, starting transfers between devices: 10.7 us -> none  [the longest x2 4.94 us: passed_along(): lax.ppermute(array, axis, [(i, (i + by) % devices) for i in range(devices)])]
  transfers between devices with their start and end apart: 5 -> 0, of which waited for: 2 -> 0; matrix products, arithmetic and copies ran while one was open for 1% -> 0% of each run, Pallas kernels for 0% -> 0%
where the time goes in v1:
time: 32.2 us; the launch traced here: 31.9 us
  Pallas kernels  29.2 us (91%)
  local copies, waits for them, and re-layouts  1.37 us (4%)
  other arithmetic  1.33 us (4%)
    pallas_call x1, Pallas kernels, per_device(): pl.pallas_call(kernel, out_shape=jax.ShapeDtypeStruct(source.shape, F32),...  29.2 us
    unnamed x3, local copies, waits for them, and re-layouts  1.37 us
    sub x1, other arithmetic, per_device(): return total - source  1.33 us

profile of v1, /device:TPU:1, one launch (start us, length us, event | category | flops | bytes accessed | tf_op | source)
XLA Modules:
  0.0 31.9 jit_solution(13856900008805469589)
XLA Ops:
  0.0 0.0 copy-start
  0.0 1.4 %copy.8.pat_hbm = s32[16,4]{1,0:T(8,128)} copy(s32[16,4]{0,1:T(4,128)} %param.9) | data formatting | bytes 512 | tf_op args[2]
  1.4 29.2 %residual.1 = f32[2,2048]{1,0:T(2,128)} custom-call(bf16[2,2048]{1,0:T(2,128)(2,1)} %coef_hbm.1, bf16[16,4,128,384]{3,2,1,0:T(8,128)(2,1)} %curl_hbm.1, s32[16,4]{1,0:T(8,128)} %copy.8.pat_hbm, s32[16]{0:T(128)} %reg_hbm.1, f32[3,4]{1,0:T(4,128)} %law_hbm.1, bf16[288,256]{1,0:T(8,128)(2,1)} %constant.2.clone.tab_hbm), custom_call_target="tpu_custom_call" | custom-call | tf_op jit(solution)/shard_map/residual/pallas_call | solution.py:249
  30.6 0.0 copy-done
  30.6 1.3 %sub.3 = f32[2,2048]{1,0:T(2,128)} subtract(f32[2,2048]{1,0:T(2,128)} %residual.1, f32[2,2048]{1,0:T(2,128)S(1)} %copy-done) | non-fusion elementwise | flops 4096 | bytes 49152 | tf_op jit(solution)/shard_map/sub | solution.py:278
Async XLA Ops:
  0.0 30.6 %copy-start = (f32[2,2048]{1,0:T(2,128)S(1)}, f32[2,2048]{1,0:T(2,128)}, u32[]{:S(2)}) copy-start(f32[2,2048]{1,0:T(2,128)} %param.12) | copy-start | bytes 49156

commit v2 on v1

--- a/solution.py
+++ b/solution.py
@@ -67,8 +67,15 @@
     def at(group, other):
         return (other // 4, group, lax.rem(other, 4))
 
-    near = [lax.rem(rank + d, GROUP) for d in range(1, GROUP)]
-    everyone = [lax.rem(rank + d, GROUP) for d in range(GROUP)]
+    place = harm // 2 * 4 + samp
+    core = lax.rem(harm, 2)
+
+    def peer(step, swap):
+        there = lax.rem(place + step, 8)
+        return (there // 4 * 2 + lax.rem(core + swap, 2)) * 4 + lax.rem(there, 4)
+
+    everyone = [peer(step, swap) for step in (4, 3, 5, 2, 6, 1, 7, 0) for swap in (1, 0)]
+    near = everyone[:-1]
     after, before = lax.rem(space + 1, SPACE), lax.rem(space + SPACE - 1, SPACE)
 
     loads = [
@@ -82,16 +89,17 @@
     for load in loads:
         load.start()
     barrier = pltpu.get_barrier_semaphore()
+    for group in (after, before):
+        for other in everyone:
+            pl.semaphore_signal(barrier, inc=1, device_id=at(group, other), device_id_type=MESH)
     for other in near:
         pl.semaphore_signal(barrier, inc=1, device_id=at(space, other), device_id_type=MESH)
-    for other in everyone:
-        for group in (after, before):
-            pl.semaphore_signal(barrier, inc=1, device_id=at(group, other), device_id_type=MESH)
 
     loads[0].wait()
     loads[1].wait()
+    pattern = pat[...].T
     rows = jnp.concatenate(
-        [jnp.broadcast_to(pat[e : e + 1, :], (2 * LINKS, LINKS)) for e in range(TILES)], axis=0
+        [jnp.broadcast_to(pattern[e : e + 1, :], (2 * LINKS, LINKS)) for e in range(TILES)], axis=0
     )
     row = lax.broadcasted_iota(jnp.int32, (TILES * LINKS * 2, LINKS), 0)
     col = lax.broadcasted_iota(jnp.int32, (TILES * LINKS * 2, LINKS), 1)
@@ -103,13 +111,11 @@
     own = jnp.concatenate([own[:, w * TILE : (w + 1) * TILE] for w in range(TILES)], axis=0)
     picked = jnp.dot(hits.astype(BF16), own.astype(BF16), preferred_element_type=F32)
     picks[...] = picked.reshape(TILES, 2 * LINKS, TILE).astype(BF16)
-    for e in range(TILES):
-        pass
     spread = hits.T.astype(BF16)
     spread = jnp.concatenate([spread, spread], axis=1)
 
     own_row = lax.broadcasted_iota(jnp.int32, (TILES, LINKS), 0) == rank
-    links = jnp.sum(jnp.where(own_row, pat[...], 0), axis=0, keepdims=True)
+    links = jnp.sum(jnp.where(own_row, pattern, 0), axis=0, keepdims=True)
     loads[2].wait()
     loads[3].wait()
     region = reg[...].reshape(1, TILES)
@@ -136,20 +142,21 @@
 
     pl.semaphore_wait(barrier, GROUP - 1 + 2 * GROUP)
 
+    first, last = coef.at[:, pl.ds(0, TILE)], coef.at[:, pl.ds((TILES - 1) * TILE, TILE)]
+    for other in everyone:
+        pltpu.make_async_remote_copy(
+            src_ref=first, dst_ref=high_got.at[rank], send_sem=send_sem.at[2],
+            recv_sem=recv_sem.at[2], device_id=at(before, other), device_id_type=MESH,
+        ).start()
+    for other in everyone:
+        pltpu.make_async_remote_copy(
+            src_ref=last, dst_ref=low_got.at[rank], send_sem=send_sem.at[1],
+            recv_sem=recv_sem.at[1], device_id=at(after, other), device_id_type=MESH,
+        ).start()
     for other in near:
         pltpu.make_async_remote_copy(
             src_ref=picks.at[other], dst_ref=got.at[rank], send_sem=send_sem.at[0],
             recv_sem=recv_sem.at[0], device_id=at(space, other), device_id_type=MESH,
-        ).start()
-    first, last = coef.at[:, pl.ds(0, TILE)], coef.at[:, pl.ds((TILES - 1) * TILE, TILE)]
-    for other in everyone:
-        pltpu.make_async_remote_copy(
-            src_ref=last, dst_ref=low_got.at[rank], send_sem=send_sem.at[1],
-            recv_sem=recv_sem.at[1], device_id=at(after, other), device_id_type=MESH,
-        ).start()
-        pltpu.make_async_remote_copy(
-            src_ref=first, dst_ref=high_got.at[rank], send_sem=send_sem.at[2],
-            recv_sem=recv_sem.at[2], device_id=at(before, other), device_id_type=MESH,
         ).start()
     got[rank] = picks[rank]
 
@@ -205,12 +212,13 @@
 
     for other in everyone:
         pltpu.make_async_remote_copy(
+            src_ref=edge_flow.at[1, other], dst_ref=low_flow.at[rank], send_sem=send_sem.at[4],
+            recv_sem=recv_sem.at[4], device_id=at(after, other), device_id_type=MESH,
+        ).start()
+    for other in everyone:
+        pltpu.make_async_remote_copy(
             src_ref=edge_flow.at[0, other], dst_ref=high_flow.at[rank], send_sem=send_sem.at[3],
             recv_sem=recv_sem.at[3], device_id=at(before, other), device_id_type=MESH,
-        ).start()
-        pltpu.make_async_remote_copy(
-            src_ref=edge_flow.at[1, other], dst_ref=low_flow.at[rank], send_sem=send_sem.at[4],
-            recv_sem=recv_sem.at[4], device_id=at(after, other), device_id_type=MESH,
         ).start()
     for other in near:
         pltpu.make_async_remote_copy(
@@ -248,13 +256,13 @@
     anywhere = pl.BlockSpec(memory_space=pltpu.HBM)
     total = pl.pallas_call(
         kernel,
-        out_shape=jax.ShapeDtypeStruct(source.shape, F32),
+        out_shape=pltpu.VMEM(source.shape, F32),
         in_specs=[anywhere] * 6,
         out_specs=pl.BlockSpec(memory_space=pltpu.VMEM),
         scratch_shapes=[
             pltpu.VMEM((2, TILES * TILE), BF16),
             pltpu.VMEM((LINKS, TILE, COMP), BF16),
-            pltpu.VMEM((TILES, LINKS), jnp.int32),
+            pltpu.VMEM((LINKS, TILES), jnp.int32),
             pltpu.VMEM((TILES,), jnp.int32),
             pltpu.VMEM((3, 4), F32),
             pltpu.VMEM((288, 256), BF16),
@@ -274,7 +282,7 @@
         ],
         compiler_params=pltpu.CompilerParams(collective_id=0, has_side_effects=True),
         name="residual",
-    )(coeffs, curl_tiles, pattern, region_ids, material_law, jnp.asarray(tables()))
+    )(coeffs, curl_tiles, pattern.T, region_ids, material_law, jnp.asarray(tables()))
     return total - source
 
 

time: 32.2 us -> 27.8 us (0.86)
  Pallas kernels: 29.2 us -> 27.1 us
  local copies, waits for them, and re-layouts: 1.37 us -> 0.01 us
  other arithmetic: 1.33 us -> 0.62 us
    pallas_call x1, Pallas kernels: 29.2 us -> 27.1 us  [per_device(): pl.pallas_call(kernel, out_shape=pltpu.VMEM(source.shape, F32), in_specs=...]
    unnamed x3 -> x2, local copies, waits for them, and re-layouts: 1.37 us -> 0.01 us
    sub x1, other arithmetic: 1.33 us -> 0.62 us  [per_device(): return total - source]
where the time goes in v2:
time: 27.8 us; the launch traced here: 27.7 us
  Pallas kernels  27.1 us (97%)
  other arithmetic  0.62 us (2%)
    pallas_call x1, Pallas kernels, per_device(): pl.pallas_call(kernel, out_shape=pltpu.VMEM(source.shape, F32), in_specs=...  27.1 us
    sub x1, other arithmetic, per_device(): return total - source  0.62 us

profile of v2, /device:TPU:1, one launch (start us, length us, event | category | flops | bytes accessed | tf_op | source)
XLA Modules:
  0.0 27.7 jit_solution(2914281237053423146)
XLA Ops:
  0.0 0.0 copy-start
  0.0 27.1 %residual.1 = f32[2,2048]{1,0:T(2,128)S(1)} custom-call(bf16[2,2048]{1,0:T(2,128)(2,1)} %coef_hbm.1, bf16[16,4,128,384]{3,2,1,0:T(8,128)(2,1)} %curl_hbm.1, s32[4,16]{1,0:T(4,128)} %bitcast.1, s32[16]{0:T(128)} %reg_hbm.1, f32[3,4]{1,0:T(4,128)} %law_hbm.1, bf16[288,256]{1,0:T(8,128)(2,1)} %constant.2.clone.tab_hbm), custom_call_target="tpu_custom_call" | custom-call | tf_op jit(solution)/shard_map/residual/pallas_call | solution.py:257
  27.1 0.0 copy-done
  27.1 0.6 %sub.3 = f32[2,2048]{1,0:T(2,128)} subtract(f32[2,2048]{1,0:T(2,128)S(1)} %residual.1, f32[2,2048]{1,0:T(2,128)S(1)} %copy-done) | non-fusion elementwise | flops 4096 | bytes 49152 | tf_op jit(solution)/shard_map/sub | solution.py:286
Async XLA Ops:
  0.0 27.1 %copy-start = (f32[2,2048]{1,0:T(2,128)S(1)}, f32[2,2048]{1,0:T(2,128)}, u32[]{:S(2)}) copy-start(f32[2,2048]{1,0:T(2,128)} %param.12) | copy-start | bytes 49156

commit v3 on v2

--- a/solution.py
+++ b/solution.py
@@ -59,7 +59,7 @@
 def kernel(
     coef_hbm, curl_hbm, pat_hbm, reg_hbm, law_hbm, tab_hbm, out_ref,
     coef, curl, pat, reg, law, tab, picks, got, low_got, high_got, sums,
-    flow, flow_got, edge_flow, low_flow, high_flow, local_sem, send_sem, recv_sem,
+    flow, flow_got, edge_flow, low_flow, high_flow, local_sem, send_sem, recv_sem, ready, firsts,
 ):
     harm, space, samp = lax.axis_index("harm"), lax.axis_index("space"), lax.axis_index("samp")
     rank = harm * 4 + samp
@@ -89,9 +89,8 @@
     for load in loads:
         load.start()
     barrier = pltpu.get_barrier_semaphore()
-    for group in (after, before):
-        for other in everyone:
-            pl.semaphore_signal(barrier, inc=1, device_id=at(group, other), device_id_type=MESH)
+    for other in everyone:
+        pl.semaphore_signal(barrier, inc=1, device_id=at(before, other), device_id_type=MESH)
     for other in near:
         pl.semaphore_signal(barrier, inc=1, device_id=at(space, other), device_id_type=MESH)
 
@@ -140,13 +139,14 @@
     back = tab[256:288, 0 : 3 * HALF]
     loads[5].wait()
 
-    pl.semaphore_wait(barrier, GROUP - 1 + 2 * GROUP)
-
+    pl.semaphore_wait(barrier, GROUP - 1 + GROUP)
+
+    pl.semaphore_signal(ready, inc=1, device_id=at(after, rank), device_id_type=MESH)
     first, last = coef.at[:, pl.ds(0, TILE)], coef.at[:, pl.ds((TILES - 1) * TILE, TILE)]
-    for other in everyone:
-        pltpu.make_async_remote_copy(
-            src_ref=first, dst_ref=high_got.at[rank], send_sem=send_sem.at[2],
-            recv_sem=recv_sem.at[2], device_id=at(before, other), device_id_type=MESH,
+    for other in near:
+        pltpu.make_async_remote_copy(
+            src_ref=first, dst_ref=firsts.at[rank], send_sem=send_sem.at[6],
+            recv_sem=recv_sem.at[6], device_id=at(space, other), device_id_type=MESH,
         ).start()
     for other in everyone:
         pltpu.make_async_remote_copy(
@@ -158,6 +158,7 @@
             src_ref=picks.at[other], dst_ref=got.at[rank], send_sem=send_sem.at[0],
             recv_sem=recv_sem.at[0], device_id=at(space, other), device_id_type=MESH,
         ).start()
+    firsts[rank] = coef[:, 0:TILE]
     got[rank] = picks[rank]
 
     def total(src, dst, i):
@@ -169,9 +170,16 @@
     done = [
         total(picks.at[pl.ds(0, GROUP - 1)], got.at[pl.ds(0, GROUP - 1)], 0),
         total(low_got, low_got, 1),
-        total(high_got, high_got, 2),
+        pltpu.make_async_remote_copy(
+            src_ref=firsts, dst_ref=high_got, send_sem=send_sem.at[2], recv_sem=recv_sem.at[2],
+            device_id=at(before, rank), device_id_type=MESH,
+        ),
+        total(firsts.at[pl.ds(0, GROUP - 1)], firsts.at[pl.ds(0, GROUP - 1)], 6),
     ]
-    for d in done:
+    done[3].wait_recv()
+    pl.semaphore_wait(ready, 1)
+    done[2].start()
+    for d in done[:3]:
         d.wait_recv()
 
     halo = [ref[...].astype(F32).reshape(PARTS, TILE).astype(BF16) for ref in (low_got, high_got)]
@@ -233,7 +241,7 @@
         total(edge_flow.at[1], low_flow, 4),
         total(flow.at[pl.ds(0, 8 * (GROUP - 1))], flow_got.at[pl.ds(0, 8 * (GROUP - 1))], 5),
     ]
-    for d in done[3:]:
+    for d in done[4:]:
         d.wait_recv()
     owned = jnp.dot(
         spread, jnp.concatenate(split(flow_got[...]), axis=0), preferred_element_type=F32
@@ -277,8 +285,10 @@
             pltpu.VMEM((GROUP, 2, TILE), F32),
             pltpu.VMEM((GROUP, 2, TILE), F32),
             pltpu.SemaphoreType.DMA((6,)),
-            pltpu.SemaphoreType.DMA((6,)),
-            pltpu.SemaphoreType.DMA((6,)),
+            pltpu.SemaphoreType.DMA((7,)),
+            pltpu.SemaphoreType.DMA((7,)),
+            pltpu.SemaphoreType.REGULAR,
+            pltpu.VMEM((GROUP, 2, TILE), BF16),
         ],
         compiler_params=pltpu.CompilerParams(collective_id=0, has_side_effects=True),
         name="residual",

time: 27.8 us -> 26.4 us (0.950)
  Pallas kernels: 27.1 us -> 25.7 us
    pallas_call x1, Pallas kernels: 27.1 us -> 25.7 us  [per_device(): pl.pallas_call(kernel, out_shape=pltpu.VMEM(source.shape, F32), in_specs=...]
where the time goes in v3:
time: 26.4 us
  Pallas kernels  25.7 us (97%)
  other arithmetic  0.62 us (2%)
    pallas_call x1, Pallas kernels, per_device(): pl.pallas_call(kernel, out_shape=pltpu.VMEM(source.shape, F32), in_specs=...  25.7 us
    sub x1, other arithmetic, per_device(): return total - source  0.62 us

profile of v3, /device:TPU:1, one launch (start us, length us, event | category | flops | bytes accessed | tf_op | source)
XLA Modules:
  0.0 26.4 jit_solution(6175231010889976512)
XLA Ops:
  0.0 0.0 copy-start
  0.0 25.7 %residual.1 = f32[2,2048]{1,0:T(2,128)S(1)} custom-call(bf16[2,2048]{1,0:T(2,128)(2,1)} %coef_hbm.1, bf16[16,4,128,384]{3,2,1,0:T(8,128)(2,1)} %curl_hbm.1, s32[4,16]{1,0:T(4,128)} %bitcast.1, s32[16]{0:T(128)} %reg_hbm.1, f32[3,4]{1,0:T(4,128)} %law_hbm.1, bf16[288,256]{1,0:T(8,128)(2,1)} %constant.2.clone.tab_hbm), custom_call_target="tpu_custom_call" | custom-call | tf_op jit(solution)/shard_map/residual/pallas_call | solution.py:265
  25.7 0.0 copy-done
  25.7 0.6 %sub.3 = f32[2,2048]{1,0:T(2,128)} subtract(f32[2,2048]{1,0:T(2,128)S(1)} %residual.1, f32[2,2048]{1,0:T(2,128)S(1)} %copy-done) | non-fusion elementwise | flops 4096 | bytes 49152 | tf_op jit(solution)/shard_map/sub | solution.py:296
Async XLA Ops:
  0.0 25.7 %copy-start = (f32[2,2048]{1,0:T(2,128)S(1)}, f32[2,2048]{1,0:T(2,128)}, u32[]{:S(2)}) copy-start(f32[2,2048]{1,0:T(2,128)} %param.12) | copy-start | bytes 49156

commit v4 on v3

--- a/solution.py
+++ b/solution.py
@@ -141,13 +141,24 @@
 
     pl.semaphore_wait(barrier, GROUP - 1 + GROUP)
 
-    pl.semaphore_signal(ready, inc=1, device_id=at(after, rank), device_id_type=MESH)
+    hub = rank - 4 * core + 4
+    pl.semaphore_signal(ready, inc=1, device_id=at(after, hub), device_id_type=MESH)
     first, last = coef.at[:, pl.ds(0, TILE)], coef.at[:, pl.ds((TILES - 1) * TILE, TILE)]
-    for other in near:
-        pltpu.make_async_remote_copy(
+
+    def to_hub(other):
+        return pltpu.make_async_remote_copy(
             src_ref=first, dst_ref=firsts.at[rank], send_sem=send_sem.at[6],
             recv_sem=recv_sem.at[6], device_id=at(space, other), device_id_type=MESH,
-        ).start()
+        )
+
+    hubs = [peer(step, 1 - core) for step in (4, 3, 5, 2, 6, 1, 7)]
+    for other in hubs:
+        to_hub(other).start()
+
+    @pl.when(core == 0)
+    def _():
+        to_hub(hub).start()
+
     for other in everyone:
         pltpu.make_async_remote_copy(
             src_ref=last, dst_ref=low_got.at[rank], send_sem=send_sem.at[1],
@@ -170,15 +181,24 @@
     done = [
         total(picks.at[pl.ds(0, GROUP - 1)], got.at[pl.ds(0, GROUP - 1)], 0),
         total(low_got, low_got, 1),
-        pltpu.make_async_remote_copy(
+        total(high_got, high_got, 2),
+    ]
+
+    def from_hub(other):
+        return pltpu.make_async_remote_copy(
             src_ref=firsts, dst_ref=high_got, send_sem=send_sem.at[2], recv_sem=recv_sem.at[2],
-            device_id=at(before, rank), device_id_type=MESH,
-        ),
-        total(firsts.at[pl.ds(0, GROUP - 1)], firsts.at[pl.ds(0, GROUP - 1)], 6),
-    ]
-    done[3].wait_recv()
-    pl.semaphore_wait(ready, 1)
-    done[2].start()
+            device_id=at(before, other), device_id_type=MESH,
+        )
+
+    gathered = total(firsts.at[pl.ds(0, GROUP - 1)], firsts.at[pl.ds(0, GROUP - 1)], 6)
+
+    @pl.when(core == 1)
+    def _():
+        gathered.wait_recv()
+        pl.semaphore_wait(ready, 2)
+        from_hub(rank - 4).start()
+        from_hub(rank).start()
+
     for d in done[:3]:
         d.wait_recv()
 
@@ -241,7 +261,7 @@
         total(edge_flow.at[1], low_flow, 4),
         total(flow.at[pl.ds(0, 8 * (GROUP - 1))], flow_got.at[pl.ds(0, 8 * (GROUP - 1))], 5),
     ]
-    for d in done[4:]:
+    for d in done[3:]:
         d.wait_recv()
     owned = jnp.dot(
         spread, jnp.concatenate(split(flow_got[...]), axis=0), preferred_element_type=F32
@@ -256,8 +276,19 @@
         if w == TILES - 1:
             piece = piece + high_sum
         out_ref[:, w * TILE : (w + 1) * TILE] = piece
-    for d in done:
+    for d in done[:2] + done[3:]:
         d.wait_send()
+    for other in hubs:
+        to_hub(other).wait_send()
+
+    @pl.when(core == 0)
+    def _():
+        to_hub(hub).wait_send()
+
+    @pl.when(core == 1)
+    def _():
+        from_hub(rank - 4).wait_send()
+        from_hub(rank).wait_send()
 
 
 def per_device(coeffs, curl_tiles, pattern, region_ids, material_law, source):

time: 26.4 us -> 25.5 us (0.966)
  Pallas kernels: 25.7 us -> 24.8 us
    pallas_call x1, Pallas kernels: 25.7 us -> 24.8 us  [per_device(): pl.pallas_call(kernel, out_shape=pltpu.VMEM(source.shape, F32), in_specs=...]
where the time goes in v4:
time: 25.5 us; the launch traced here: 25.4 us
  Pallas kernels  24.8 us (97%)
  other arithmetic  0.62 us (2%)
    pallas_call x1, Pallas kernels, per_device(): pl.pallas_call(kernel, out_shape=pltpu.VMEM(source.shape, F32), in_specs=...  24.8 us
    sub x1, other arithmetic, per_device(): return total - source  0.62 us

profile of v4, /device:TPU:1, one launch (start us, length us, event | category | flops | bytes accessed | tf_op | source)
XLA Modules:
  0.0 25.4 jit_solution(8877592690665759585)
XLA Ops:
  0.0 0.0 copy-start
  0.0 24.8 %residual.1 = f32[2,2048]{1,0:T(2,128)S(1)} custom-call(bf16[2,2048]{1,0:T(2,128)(2,1)} %coef_hbm.1, bf16[16,4,128,384]{3,2,1,0:T(8,128)(2,1)} %curl_hbm.1, s32[4,16]{1,0:T(4,128)} %bitcast.1, s32[16]{0:T(128)} %reg_hbm.1, f32[3,4]{1,0:T(4,128)} %law_hbm.1, bf16[288,256]{1,0:T(8,128)(2,1)} %constant.2.clone.tab_hbm), custom_call_target="tpu_custom_call" | custom-call | tf_op jit(solution)/shard_map/residual/pallas_call | solution.py:296
  24.8 0.0 copy-done
  24.8 0.6 %sub.3 = f32[2,2048]{1,0:T(2,128)} subtract(f32[2,2048]{1,0:T(2,128)S(1)} %residual.1, f32[2,2048]{1,0:T(2,128)S(1)} %copy-done) | non-fusion elementwise | flops 4096 | bytes 49152 | tf_op jit(solution)/shard_map/sub | solution.py:327
Async XLA Ops:
  0.0 24.8 %copy-start = (f32[2,2048]{1,0:T(2,128)S(1)}, f32[2,2048]{1,0:T(2,128)}, u32[]{:S(2)}) copy-start(f32[2,2048]{1,0:T(2,128)} %param.12) | copy-start | bytes 49156

commit v5 on v2

v5 whole, which is shorter than its diff:
```python
import math

import jax
import jax.numpy as jnp
import ml_dtypes
import numpy as np
from jax import lax
from jax.experimental import pallas as pl
from jax.experimental.pallas import tpu as pltpu
from jax.sharding import PartitionSpec as P

SAMPLES = 64
HALF = SAMPLES // 2
PARTS = 32
GROUP = 16
HUBS = 8
OWN = 2
SPACE = 16
TILES = 16
LINKS = 4
TILE = 128
COMP = 3 * TILE
ROWS = OWN * LINKS * 2
WAVES = OWN * LINKS * HALF
MESH = pl.DeviceIdType.MESH
F32, BF16 = jnp.float32, jnp.bfloat16


def two_pieces(table):
    high = table.astype(ml_dtypes.bfloat16)
    low = (table - high.astype(np.float64)).astype(ml_dtypes.bfloat16)
    return high, low


def tables():
    t = np.arange(HALF)[:, None]
    q = np.arange(PARTS)[None, :]
    phase = ((2 * (q // 2) + 1) * t % SAMPLES) * (2.0 * math.pi / SAMPLES)
    transform = np.where(q % 2 == 0, np.cos(phase), np.sin(phase))
    by_rank = transform.reshape(HALF, GROUP, 2)
    main = np.zeros((OWN, LINKS, HALF, GROUP, OWN, LINKS, 2))
    for v in range(OWN):
        for k in range(LINKS):
            main[v, k, :, :, v, k, :] = by_rank
    main = main.reshape(WAVES, GROUP * ROWS)
    halo = np.zeros((HALF, GROUP * ROWS))
    halo[:, : 2 * PARTS] = np.tile(transform, (1, 2))
    back = (4.0 / SAMPLES) * by_rank.transpose(2, 1, 0).reshape(PARTS, HALF)
    back_high, back_low = two_pieces(back)
    back_row = np.zeros((PARTS, GROUP * ROWS), ml_dtypes.bfloat16)
    back_row[:, : 3 * HALF] = np.concatenate([back_high, back_low, back_high], axis=1)
    return np.concatenate([*two_pieces(main), *two_pieces(halo), back_row], axis=0)


def split(value):
    high = value.astype(BF16)
    return high, (value - high.astype(F32)).astype(BF16)


def kernel(
    coef_hbm, curl_hbm, pat_hbm, reg_hbm, law_hbm, tab_hbm, out_ref,
    coef, curl, pat, reg, law, tab, halo_tab, picks, got, firsts, low_got, high_got,
    flow, flow_got, edge_flow, low_flow, high_flow, local_sem, send_sem, recv_sem, ready,
):
    harm, space, samp = lax.axis_index("harm"), lax.axis_index("space"), lax.axis_index("samp")
    rank = harm * 4 + samp
    place = harm // 2 * 4 + samp
    core = lax.rem(harm, 2)
    after, before = lax.rem(space + 1, SPACE), lax.rem(space + SPACE - 1, SPACE)

    def rank_at(z, c):
        return (z // 4 * 2 + c) * 4 + lax.rem(z, 4)

    def at(group, other):
        return (other // 4, group, lax.rem(other, 4))

    far = [lax.rem(place + step, 8) for step in (4, 3, 5, 2, 6, 1, 7)]
    hubs = [(z, rank_at(z, 1)) for z in far]
    home = rank_at(place, 1)
    everyone = [rank_at(z, c) for z in far + [place] for c in (1 - core, core)]
    near = everyone[:-1]

    loads = [
        pltpu.make_async_copy(coef_hbm, coef, local_sem.at[0]),
        pltpu.make_async_copy(pat_hbm, pat, local_sem.at[1]),
        pltpu.make_async_copy(reg_hbm, reg, local_sem.at[2]),
        pltpu.make_async_copy(law_hbm, law, local_sem.at[3]),
        pltpu.make_async_copy(tab_hbm, tab, local_sem.at[4]),
        pltpu.make_async_copy(curl_hbm.at[pl.ds(OWN * place, OWN)], curl, local_sem.at[5]),
    ]
    for load in loads[:4]:
        load.start()
    barrier = pltpu.get_barrier_semaphore()

    @pl.when(core == 1)
    def _():
        for other in near:
            pl.semaphore_signal(barrier, inc=1, device_id=at(space, other), device_id_type=MESH)
        for other in everyone:
            pl.semaphore_signal(barrier, inc=1, device_id=at(before, other), device_id_type=MESH)
        for load in loads[4:]:
            load.start()

    loads[0].wait()
    loads[1].wait()
    pattern = pat[...].T
    rows = jnp.concatenate(
        [jnp.broadcast_to(pattern[e : e + 1, :], (2 * LINKS, LINKS)) for e in range(TILES)], axis=0
    )
    row = lax.broadcasted_iota(jnp.int32, (TILES * LINKS * 2, LINKS), 0)
    col = lax.broadcasted_iota(jnp.int32, (TILES * LINKS * 2, LINKS), 1)
    spot = jnp.sum(jnp.where(row // 2 % LINKS == col, rows, 0), axis=1, keepdims=True)
    row = lax.broadcasted_iota(jnp.int32, (TILES * LINKS * 2, TILES * 2), 0)
    col = lax.broadcasted_iota(jnp.int32, (TILES * LINKS * 2, TILES * 2), 1)
    hits = jnp.where((spot == col // 2 + 1) & (row % 2 == col % 2), 1.0, 0.0)
    own = coef[...].astype(F32)
    own = jnp.concatenate([own[:, w * TILE : (w + 1) * TILE] for w in range(TILES)], axis=0)
    picked = jnp.dot(hits.astype(BF16), own.astype(BF16), preferred_element_type=F32)
    picks[...] = picked.reshape(HUBS, ROWS, TILE).astype(BF16)
    spread = hits.T.astype(BF16)
    spread = jnp.concatenate([spread, spread], axis=1)

    loads[2].wait()
    loads[3].wait()
    links, laws = [], []
    for v in range(OWN):
        element = OWN * place + v
        own_row = lax.broadcasted_iota(jnp.int32, (TILES, LINKS), 0) == element
        links.append(jnp.sum(jnp.where(own_row, pattern, 0), axis=0, keepdims=True))
        region = reg[...].reshape(1, TILES)
        lane = lax.broadcasted_iota(jnp.int32, (1, TILES), 1)
        region = jnp.sum(jnp.where(lane == element, region, 0), axis=1, keepdims=True)
        lane = lax.broadcasted_iota(jnp.int32, (3, 4), 1)
        own_law = jnp.sum(jnp.where(lane == region, law[...], 0.0), axis=1, keepdims=True)
        laws.append((own_law[0:1], own_law[1:2], own_law[2:3]))

    @pl.when(core == 1)
    def _():
        loads[4].wait()
        lane = lax.broadcasted_iota(jnp.int32, (1, 2 * PARTS), 1)
        side = jnp.where(lane < PARTS, 0, TILES + 1)
        for piece in range(2):
            at_row = 2 * WAVES + piece * HALF
            plain = tab[at_row : at_row + HALF, 0 : 2 * PARTS].astype(F32)
            for v in range(OWN):
                for k in range(LINKS):
                    mask = jnp.where(links[v][:, k : k + 1] == side, 1.0, 0.0)
                    to_row = ((piece * OWN + v) * LINKS + k) * HALF
                    halo_tab[to_row : to_row + HALF, :] = (plain * mask).astype(BF16)
        loads[5].wait()

    def remote(src, dst, i, group, other):
        return pltpu.make_async_remote_copy(
            src_ref=src, dst_ref=dst, send_sem=send_sem.at[i], recv_sem=recv_sem.at[i],
            device_id=at(group, other), device_id_type=MESH,
        )

    pl.semaphore_wait(barrier, GROUP - core)

    @pl.when(core == 1)
    def _():
        pl.semaphore_signal(ready, inc=1, device_id=at(after, rank), device_id_type=MESH)

    first, last = coef.at[:, pl.ds(0, TILE)], coef.at[:, pl.ds((TILES - 1) * TILE, TILE)]
    sent_first = [remote(first, firsts.at[rank], 0, space, other) for _, other in hubs]
    sent_last = [remote(last, low_got.at[rank], 1, after, other) for _, other in hubs]
    sent_last.append(remote(last, low_got.at[rank], 1, after, home))
    sent_picks = [remote(picks.at[z], got.at[rank], 3, space, other) for z, other in hubs]
    home_first = remote(first, firsts.at[rank], 0, space, home)
    home_picks = remote(picks.at[place], got.at[rank], 3, space, home)
    for copy in sent_first:
        copy.start()

    @pl.when(core == 0)
    def _():
        home_first.start()

    for copy in sent_last + sent_picks:
        copy.start()

    @pl.when(core == 0)
    def _():
        home_picks.start()

    def block(ref, which):
        return ref.at[pl.ds(pl.multiple_of(which * ROWS, ROWS), ROWS)]

    @pl.when(core == 1)
    def _():
        firsts[rank] = coef[:, 0:TILE]
        got[rank] = picks[place]
        gathered = remote(
            firsts.at[pl.ds(0, GROUP - 1)], firsts.at[pl.ds(0, GROUP - 1)], 0, space, hubs[0][1]
        )
        gathered.wait_recv()
        pl.semaphore_wait(ready, 1)
        handed = remote(firsts, high_got, 2, before, rank)
        handed.start()
        picked = got.at[pl.ds(0, GROUP - 1)]
        remote(picked, picked, 3, space, hubs[0][1]).wait_recv()
        window = got[...].reshape(GROUP * ROWS, TILE)
        waves = jnp.dot(tab[0 : 2 * WAVES, :], window, preferred_element_type=F32)
        remote(low_got, low_got, 1, space, hubs[0][1]).wait_recv()
        handed.wait_recv()
        halo = [
            ref[...].astype(F32).reshape(PARTS, TILE).astype(BF16) for ref in (low_got, high_got)
        ]
        waves = waves + jnp.dot(
            halo_tab[...], jnp.concatenate(halo, axis=0), preferred_element_type=F32
        )
        waves = waves[:WAVES] + waves[WAVES:]
        fields, blocks = [], []
        for v in range(OWN):
            wave = jnp.concatenate(
                [
                    waves[(v * LINKS + k) * HALF : (v * LINKS + k + 1) * HALF]
                    for k in range(LINKS)
                ],
                axis=1,
            )
            blocks.append(curl[v].reshape(LINKS * TILE, COMP))
            density = jnp.dot(
                jnp.concatenate(split(wave), axis=0), blocks[v], preferred_element_type=F32
            )
            density = density[:HALF] + density[HALF:]
            comps = [density[:, c * TILE : (c + 1) * TILE] for c in range(3)]
            square = comps[0] * comps[0] + comps[1] * comps[1] + comps[2] * comps[2]
            base, knee, rise = laws[v]
            reluct = base + rise * square / (square + knee)
            fields += [reluct * c for c in comps]
        high, low = split(jnp.concatenate(fields, axis=1))
        back = tab[2 * WAVES + 2 * HALF : 2 * WAVES + 2 * HALF + PARTS, 0 : 3 * HALF]
        harmonic = jnp.dot(
            back, jnp.concatenate([high, high, low], axis=0), preferred_element_type=F32
        ).astype(BF16)
        edges = [jnp.zeros((PARTS, TILE), F32), jnp.zeros((PARTS, TILE), F32)]
        for v in range(OWN):
            contrib = lax.dot_general(
                harmonic[:, v * COMP : (v + 1) * COMP],
                blocks[v],
                (((1,), (1,)), ((), ())),
                preferred_element_type=F32,
            )
            for k in range(LINKS):
                tile = contrib[:, k * TILE : (k + 1) * TILE]
                for p in range(2):
                    flow[pl.ds((v * LINKS + k) * 2 + p, GROUP, stride=ROWS), :] = tile[
                        p * GROUP : (p + 1) * GROUP
                    ]
                for i, spot in enumerate((0, TILES + 1)):
                    edges[i] = edges[i] + jnp.where(links[v][:, k : k + 1] == spot, tile, 0.0)
        for i in range(2):
            for p in range(2):
                edge_flow[i, :, p, :] = edges[i][p * GROUP : (p + 1) * GROUP]

        to_after = [remote(edge_flow.at[1, o], low_flow.at[place], 4, after, o) for o in everyone]
        to_before = [remote(edge_flow.at[0, o], high_flow.at[place], 5, before, o) for o in everyone]
        to_group = [remote(block(flow, o), block(flow_got, place), 6, space, o) for o in near]
        for copy in to_after + to_group + to_before:
            copy.start()
        mine = pl.ds(pl.multiple_of(place * ROWS, ROWS), ROWS)
        flow_got[mine, :] = flow[pl.ds(pl.multiple_of(rank * ROWS, ROWS), ROWS), :]
        others = pl.ds(0, (HUBS - 1) * ROWS)
        remote(flow_got.at[others], flow_got.at[others], 6, space, hubs[0][1]).wait_recv()
        for copy in to_after + to_group + to_before:
            copy.wait_send()
        handed.wait_send()

    @pl.when(core == 0)
    def _():
        remote(flow_got, flow_got, 6, space, hubs[0][1]).wait_recv()

    remote(low_flow, low_flow, 4, space, hubs[0][1]).wait_recv()
    remote(high_flow, high_flow, 5, space, hubs[0][1]).wait_recv()
    owned = jnp.dot(
        spread, jnp.concatenate(split(flow_got[...]), axis=0), preferred_element_type=F32
    )
    low_sum, high_sum = low_flow[0], high_flow[0]
    for u in range(1, HUBS):
        low_sum, high_sum = low_sum + low_flow[u], high_sum + high_flow[u]
    for w in range(TILES):
        piece = owned[2 * w : 2 * w + 2]
        if w == 0:
            piece = piece + low_sum
        if w == TILES - 1:
            piece = piece + high_sum
        out_ref[:, w * TILE : (w + 1) * TILE] = piece
    for copy in sent_first + sent_last + sent_picks:
        copy.wait_send()

    @pl.when(core == 0)
    def _():
        home_first.wait_send()
        home_picks.wait_send()


def per_device(coeffs, curl_tiles, pattern, region_ids, material_law, source):
    anywhere = pl.BlockSpec(memory_space=pltpu.HBM)
    table = tables()
    total = pl.pallas_call(
        kernel,
        out_shape=pltpu.VMEM(source.shape, F32),
        in_specs=[anywhere] * 6,
        out_specs=pl.BlockSpec(memory_space=pltpu.VMEM),
        scratch_shapes=[
            pltpu.VMEM((2, TILES * TILE), BF16),
            pltpu.VMEM((OWN, LINKS, TILE, COMP), BF16),
            pltpu.VMEM((LINKS, TILES), jnp.int32),
            pltpu.VMEM((TILES,), jnp.int32),
            pltpu.VMEM((3, 4), F32),
            pltpu.VMEM(table.shape, BF16),
            pltpu.VMEM((2 * WAVES, 2 * PARTS), BF16),
            pltpu.VMEM((HUBS, ROWS, TILE), BF16),
            pltpu.VMEM((GROUP, ROWS, TILE), BF16),
            pltpu.VMEM((GROUP, 2, TILE), BF16),
            pltpu.VMEM((GROUP, 2, TILE), BF16),
            pltpu.VMEM((GROUP, 2, TILE), BF16),
            pltpu.VMEM((GROUP * ROWS, TILE), F32),
            pltpu.VMEM((HUBS * ROWS, TILE), F32),
            pltpu.VMEM((2, GROUP, 2, TILE), F32),
            pltpu.VMEM((HUBS, 2, TILE), F32),
            pltpu.VMEM((HUBS, 2, TILE), F32),
            pltpu.SemaphoreType.DMA((6,)),
            pltpu.SemaphoreType.DMA((7,)),
            pltpu.SemaphoreType.DMA((7,)),
            pltpu.SemaphoreType.REGULAR,
        ],
        compiler_params=pltpu.CompilerParams(collective_id=0, has_side_effects=True),
        name="residual",
    )(coeffs, curl_tiles, pattern.T, region_ids, material_law, jnp.asarray(table))
    return total - source


def solution(mesh):
    placed = (
        P(("harm", "samp"), "space"),
        P("space", None, None, None),
        P("space", None),
        P("space"),
        P(),
        P(("harm", "samp"), "space"),
    )
    return jax.shard_map(
        per_device,
        mesh=mesh,
        in_specs=placed,
        out_specs=P(("harm", "samp"), "space"),
        check_vma=False,
    )
```

time: 27.8 us -> 24.7 us (0.89)
  Pallas kernels: 27.1 us -> 23.9 us
    pallas_call x1, Pallas kernels: 27.1 us -> 23.9 us  [per_device(): pl.pallas_call(kernel, out_shape=pltpu.VMEM(source.shape, F32), in_specs=...]
where the time goes in v5:
time: 24.7 us; the launch traced here: 24.5 us
  Pallas kernels  23.9 us (97%)
  other arithmetic  0.62 us (3%)
    pallas_call x1, Pallas kernels, per_device(): pl.pallas_call(kernel, out_shape=pltpu.VMEM(source.shape, F32), in_specs=...  23.9 us
    sub x1, other arithmetic, per_device(): return total - source  0.62 us

profile of v5, /device:TPU:1, one launch (start us, length us, event | category | flops | bytes accessed | tf_op | source)
XLA Modules:
  0.0 24.5 jit_solution(433087907020318140)
XLA Ops:
  0.0 0.0 copy-start
  0.0 23.9 %residual.1 = f32[2,2048]{1,0:T(2,128)S(1)} custom-call(bf16[2,2048]{1,0:T(2,128)(2,1)} %coef_hbm.1, bf16[16,4,128,384]{3,2,1,0:T(8,128)(2,1)} %curl_hbm.1, s32[4,16]{1,0:T(4,128)} %bitcast.1, s32[16]{0:T(128)} %reg_hbm.1, f32[3,4]{1,0:T(4,128)} %law_hbm.1, bf16[608,256]{1,0:T(8,128)(2,1)} %constant.2.clone.tab_hbm), custom_call_target="tpu_custom_call" | custom-call | tf_op jit(solution)/shard_map/residual/pallas_call | solution.py:300
  23.9 0.0 copy-done
  23.9 0.6 %sub.3 = f32[2,2048]{1,0:T(2,128)} subtract(f32[2,2048]{1,0:T(2,128)S(1)} %residual.1, f32[2,2048]{1,0:T(2,128)S(1)} %copy-done) | non-fusion elementwise | flops 4096 | bytes 49152 | tf_op jit(solution)/shard_map/sub | solution.py:331
Async XLA Ops:
  0.0 23.9 %copy-start = (f32[2,2048]{1,0:T(2,128)S(1)}, f32[2,2048]{1,0:T(2,128)}, u32[]{:S(2)}) copy-start(f32[2,2048]{1,0:T(2,128)} %param.12) | copy-start | bytes 49156

commit v6 on v5

v6 whole, which is shorter than its diff:
```python
import math

import jax
import jax.numpy as jnp
import ml_dtypes
import numpy as np
from jax import lax
from jax.experimental import pallas as pl
from jax.experimental.pallas import tpu as pltpu
from jax.sharding import PartitionSpec as P

SAMPLES = 64
HALF = SAMPLES // 2
PARTS = 32
GROUP = 16
HUBS = 4
HUB = 4
OWN = 4
SPACE = 16
TILES = 16
LINKS = 4
TILE = 128
COMP = 3 * TILE
EDGE = LINKS * 2
ROWS = OWN * EDGE
WAVES = LINKS * HALF
MESH = pl.DeviceIdType.MESH
F32, BF16 = jnp.float32, jnp.bfloat16


def two_pieces(table):
    high = table.astype(ml_dtypes.bfloat16)
    low = (table - high.astype(np.float64)).astype(ml_dtypes.bfloat16)
    return high, low


def tables():
    t = np.arange(HALF)[:, None]
    q = np.arange(PARTS)[None, :]
    phase = ((2 * (q // 2) + 1) * t % SAMPLES) * (2.0 * math.pi / SAMPLES)
    transform = np.where(q % 2 == 0, np.cos(phase), np.sin(phase))
    by_rank = transform.reshape(HALF, GROUP, 2)
    main = np.zeros((LINKS, HALF, GROUP, LINKS, 2))
    for k in range(LINKS):
        main[k, :, :, k, :] = by_rank
    main = main.reshape(WAVES, TILE)
    halo = np.zeros((2, 2 * HALF, TILE), ml_dtypes.bfloat16)
    for side in range(2):
        halo[side, :, side * PARTS : (side + 1) * PARTS] = np.concatenate(two_pieces(transform))
    back = (4.0 / SAMPLES) * by_rank.transpose(2, 1, 0).reshape(PARTS, HALF)
    back_high, back_low = two_pieces(back)
    back_row = np.zeros((PARTS, TILE), ml_dtypes.bfloat16)
    back_row[:, : 3 * HALF] = np.concatenate([back_high, back_low, back_high], axis=1)
    return np.concatenate([*two_pieces(main), halo.reshape(4 * HALF, TILE), back_row], axis=0)


def split(value):
    high = value.astype(BF16)
    return high, (value - high.astype(F32)).astype(BF16)


def kernel(
    coef_hbm, curl_hbm, pat_hbm, reg_hbm, law_hbm, tab_hbm, out_ref,
    coef, curl, pat, reg, law, tab, picks, got, firsts, low_got, high_got,
    flow, flow_got, edge_flow, low_flow, high_flow, local_sem, send_sem, recv_sem, ready,
):
    harm, space, samp = lax.axis_index("harm"), lax.axis_index("space"), lax.axis_index("samp")
    rank = harm * 4 + samp
    is_hub = harm == 1
    after, before = lax.rem(space + 1, SPACE), lax.rem(space + SPACE - 1, SPACE)

    def at(group, other):
        if isinstance(other, int):
            return (other // 4, group, other % 4)
        return (other // 4, group, lax.rem(other, 4))

    home = HUB + samp
    hubs = [HUB + lax.rem(samp + d, HUBS) for d in range(1, HUBS)]
    launched = [(z // 4 * 2 + c) * 4 + z % 4 for z in range(8) for c in (1, 0)]
    plain = [other for other in launched if other // 4 != 1]

    loads = [
        pltpu.make_async_copy(coef_hbm, coef, local_sem.at[0]),
        pltpu.make_async_copy(pat_hbm, pat, local_sem.at[1]),
        pltpu.make_async_copy(reg_hbm, reg, local_sem.at[2]),
        pltpu.make_async_copy(law_hbm, law, local_sem.at[3]),
        pltpu.make_async_copy(tab_hbm, tab, local_sem.at[4]),
        pltpu.make_async_copy(curl_hbm.at[pl.ds(OWN * samp, OWN)], curl, local_sem.at[5]),
    ]
    for load in loads[:4]:
        load.start()
    barrier = pltpu.get_barrier_semaphore()

    @pl.when(is_hub)
    def _():
        for group, others in ((space, hubs), (before, [*hubs, home]), (space, plain), (before, plain)):
            for other in others:
                pl.semaphore_signal(barrier, inc=1, device_id=at(group, other), device_id_type=MESH)
        for load in loads[4:]:
            load.start()

    loads[0].wait()
    loads[1].wait()
    pattern = pat[...].T
    rows = jnp.concatenate(
        [jnp.broadcast_to(pattern[e : e + 1, :], (2 * LINKS, LINKS)) for e in range(TILES)], axis=0
    )
    row = lax.broadcasted_iota(jnp.int32, (TILES * LINKS * 2, LINKS), 0)
    col = lax.broadcasted_iota(jnp.int32, (TILES * LINKS * 2, LINKS), 1)
    spot = jnp.sum(jnp.where(row // 2 % LINKS == col, rows, 0), axis=1, keepdims=True)
    row = lax.broadcasted_iota(jnp.int32, (TILES * LINKS * 2, TILES * 2), 0)
    col = lax.broadcasted_iota(jnp.int32, (TILES * LINKS * 2, TILES * 2), 1)
    hits = jnp.where((spot == col // 2 + 1) & (row % 2 == col % 2), 1.0, 0.0)
    own = coef[...].astype(F32)
    own = jnp.concatenate([own[:, w * TILE : (w + 1) * TILE] for w in range(TILES)], axis=0)
    picked = jnp.dot(hits.astype(BF16), own.astype(BF16), preferred_element_type=F32)
    picks[...] = picked.reshape(HUBS, OWN, EDGE, TILE).astype(BF16)
    spread = hits.T.astype(BF16)
    spread = jnp.concatenate([spread, spread], axis=1)

    loads[2].wait()
    loads[3].wait()
    links, laws = [], []
    for v in range(OWN):
        element = OWN * samp + v
        own_row = lax.broadcasted_iota(jnp.int32, (TILES, LINKS), 0) == element
        links.append(jnp.sum(jnp.where(own_row, pattern, 0), axis=0, keepdims=True))
        region = reg[...].reshape(1, TILES)
        lane = lax.broadcasted_iota(jnp.int32, (1, TILES), 1)
        region = jnp.sum(jnp.where(lane == element, region, 0), axis=1, keepdims=True)
        lane = lax.broadcasted_iota(jnp.int32, (3, 4), 1)
        own_law = jnp.sum(jnp.where(lane == region, law[...], 0.0), axis=1, keepdims=True)
        laws.append((own_law[0:1], own_law[1:2], own_law[2:3]))

    @pl.when(is_hub)
    def _():
        loads[4].wait()
        loads[5].wait()

    def remote(src, dst, i, group, other):
        return pltpu.make_async_remote_copy(
            src_ref=src, dst_ref=dst, send_sem=send_sem.at[i], recv_sem=recv_sem.at[i],
            device_id=at(group, other), device_id_type=MESH,
        )

    pl.semaphore_wait(barrier, jnp.where(is_hub, 2 * HUBS - 1, 2 * HUBS))

    @pl.when(is_hub)
    def _():
        pl.semaphore_signal(ready, inc=1, device_id=at(after, rank), device_id_type=MESH)

    first, last = coef.at[:, pl.ds(0, TILE)], coef.at[:, pl.ds((TILES - 1) * TILE, TILE)]
    sent_first = [remote(first, firsts.at[rank], 0, space, other) for other in hubs]
    sent_last = [remote(last, low_got.at[rank], 1, after, other) for other in [home, *hubs]]
    sent_picks = [remote(picks.at[other - HUB], got.at[rank], 3, space, other) for other in hubs]
    home_first = remote(first, firsts.at[rank], 0, space, home)
    home_picks = remote(picks.at[samp], got.at[rank], 3, space, home)

    @pl.when(jnp.logical_not(is_hub))
    def _():
        home_first.start()

    for copy in sent_first + sent_last:
        copy.start()

    @pl.when(jnp.logical_not(is_hub))
    def _():
        home_picks.start()

    for copy in sent_picks:
        copy.start()

    def block(ref, which):
        start = which * ROWS if isinstance(which, int) else pl.multiple_of(which * ROWS, ROWS)
        return ref.at[pl.ds(start, ROWS)]

    @pl.when(is_hub)
    def _():
        firsts[rank] = coef[:, 0:TILE]
        got[rank] = picks[samp]
        gathered = firsts.at[pl.ds(0, GROUP - 1)]
        remote(gathered, gathered, 0, space, hubs[0]).wait_recv()
        pl.semaphore_wait(ready, 1)
        handed = remote(firsts, high_got, 2, before, rank)
        handed.start()
        picked = got.at[pl.ds(0, GROUP - 1)]
        remote(picked, picked, 3, space, hubs[0]).wait_recv()
        waves = []
        for v in range(OWN):
            window = got[:, v].reshape(GROUP * EDGE, TILE)
            wave = jnp.dot(tab[0 : 2 * WAVES, :], window, preferred_element_type=F32)
            waves.append(wave[:WAVES] + wave[WAVES:])
        remote(low_got, low_got, 1, space, hubs[0]).wait_recv()
        handed.wait_recv()
        halo = [
            ref[...].astype(F32).reshape(PARTS, TILE).astype(BF16) for ref in (low_got, high_got)
        ]
        halo = jnp.dot(
            tab[2 * WAVES : 2 * WAVES + 4 * HALF, 0 : 2 * PARTS],
            jnp.concatenate(halo, axis=0),
            preferred_element_type=F32,
        )
        halo = [halo[2 * i * HALF :][:HALF] + halo[(2 * i + 1) * HALF :][:HALF] for i in range(2)]
        back = tab[2 * WAVES + 4 * HALF : 2 * WAVES + 4 * HALF + PARTS, 0 : 3 * HALF]
        edges = [jnp.zeros((PARTS, TILE), F32), jnp.zeros((PARTS, TILE), F32)]
        for v in range(OWN):
            wave = []
            for k in range(LINKS):
                piece = waves[v][k * HALF : (k + 1) * HALF]
                for i, spot in enumerate((0, TILES + 1)):
                    piece = piece + jnp.where(links[v][:, k : k + 1] == spot, halo[i], 0.0)
                wave.append(piece)
            blocks = curl[v].reshape(LINKS * TILE, COMP)
            density = jnp.dot(
                jnp.concatenate(split(jnp.concatenate(wave, axis=1)), axis=0),
                blocks,
                preferred_element_type=F32,
            )
            density = density[:HALF] + density[HALF:]
            comps = [density[:, c * TILE : (c + 1) * TILE] for c in range(3)]
            square = comps[0] * comps[0] + comps[1] * comps[1] + comps[2] * comps[2]
            base, knee, rise = laws[v]
            reluct = base + rise * square / (square + knee)
            high, low = split(jnp.concatenate([reluct * c for c in comps], axis=1))
            harmonic = jnp.dot(
                back, jnp.concatenate([high, high, low], axis=0), preferred_element_type=F32
            )
            contrib = lax.dot_general(
                harmonic.astype(BF16), blocks, (((1,), (1,)), ((), ())), preferred_element_type=F32
            )
            for k in range(LINKS):
                tile = contrib[:, k * TILE : (k + 1) * TILE]
                for p in range(2):
                    flow[pl.ds(v * EDGE + 2 * k + p, GROUP, stride=ROWS), :] = tile[
                        p * GROUP : (p + 1) * GROUP
                    ]
                for i, spot in enumerate((0, TILES + 1)):
                    edges[i] = edges[i] + jnp.where(links[v][:, k : k + 1] == spot, tile, 0.0)
        for i in range(2):
            for p in range(2):
                edge_flow[i, :, p, :] = edges[i][p * GROUP : (p + 1) * GROUP]

        to_after = [remote(edge_flow.at[1, o], low_flow.at[samp], 4, after, o) for o in launched]
        to_before = [remote(edge_flow.at[0, o], high_flow.at[samp], 5, before, o) for o in launched]
        to_group = [remote(block(flow, o), block(flow_got, samp), 6, space, o) for o in launched]
        for other, *copies in zip(launched, to_after, to_group, to_before):
            copies[0].start()

            @pl.when(rank != other)
            def _():
                copies[1].start()

            copies[2].start()
        mine = pl.ds(pl.multiple_of(samp * ROWS, ROWS), ROWS)
        flow_got[mine, :] = flow[pl.ds(pl.multiple_of(rank * ROWS, ROWS), ROWS), :]
        others = pl.ds(0, (HUBS - 1) * ROWS)
        remote(flow_got.at[others], flow_got.at[others], 6, space, hubs[0]).wait_recv()

    @pl.when(jnp.logical_not(is_hub))
    def _():
        remote(flow_got, flow_got, 6, space, home).wait_recv()

    remote(low_flow, low_flow, 4, after, home).wait_recv()
    remote(high_flow, high_flow, 5, after, home).wait_recv()
    owned = jnp.dot(
        spread, jnp.concatenate(split(flow_got[...]), axis=0), preferred_element_type=F32
    )
    low_sum, high_sum = low_flow[0], high_flow[0]
    for u in range(1, HUBS):
        low_sum, high_sum = low_sum + low_flow[u], high_sum + high_flow[u]
    for w in range(TILES):
        piece = owned[2 * w : 2 * w + 2]
        if w == 0:
            piece = piece + low_sum
        if w == TILES - 1:
            piece = piece + high_sum
        out_ref[:, w * TILE : (w + 1) * TILE] = piece
    for copy in sent_first + sent_last + sent_picks:
        copy.wait_send()

    @pl.when(jnp.logical_not(is_hub))
    def _():
        home_first.wait_send()
        home_picks.wait_send()

    @pl.when(is_hub)
    def _():
        others = pl.ds(0, (GROUP - 1) * ROWS)
        remote(firsts, high_got, 2, before, rank).wait_send()
        remote(edge_flow.at[1], edge_flow.at[1], 4, after, home).wait_send()
        remote(edge_flow.at[0], edge_flow.at[0], 5, after, home).wait_send()
        remote(flow.at[others], flow.at[others], 6, after, home).wait_send()


def per_device(coeffs, curl_tiles, pattern, region_ids, material_law, source):
    anywhere = pl.BlockSpec(memory_space=pltpu.HBM)
    table = tables()
    total = pl.pallas_call(
        kernel,
        out_shape=pltpu.VMEM(source.shape, F32),
        in_specs=[anywhere] * 6,
        out_specs=pl.BlockSpec(memory_space=pltpu.VMEM),
        scratch_shapes=[
            pltpu.VMEM((2, TILES * TILE), BF16),
            pltpu.VMEM((OWN, LINKS, TILE, COMP), BF16),
            pltpu.VMEM((LINKS, TILES), jnp.int32),
            pltpu.VMEM((TILES,), jnp.int32),
            pltpu.VMEM((3, 4), F32),
            pltpu.VMEM(table.shape, BF16),
            pltpu.VMEM((HUBS, OWN, EDGE, TILE), BF16),
            pltpu.VMEM((GROUP, OWN, EDGE, TILE), BF16),
            pltpu.VMEM((GROUP, 2, TILE), BF16),
            pltpu.VMEM((GROUP, 2, TILE), BF16),
            pltpu.VMEM((GROUP, 2, TILE), BF16),
            pltpu.VMEM((GROUP * ROWS, TILE), F32),
            pltpu.VMEM((HUBS * ROWS, TILE), F32),
            pltpu.VMEM((2, GROUP, 2, TILE), F32),
            pltpu.VMEM((HUBS, 2, TILE), F32),
            pltpu.VMEM((HUBS, 2, TILE), F32),
            pltpu.SemaphoreType.DMA((6,)),
            pltpu.SemaphoreType.DMA((7,)),
            pltpu.SemaphoreType.DMA((7,)),
            pltpu.SemaphoreType.REGULAR,
        ],
        compiler_params=pltpu.CompilerParams(collective_id=0, has_side_effects=True),
        name="residual",
    )(coeffs, curl_tiles, pattern.T, region_ids, material_law, jnp.asarray(table))
    return total - source


def solution(mesh):
    placed = (
        P(("harm", "samp"), "space"),
        P("space", None, None, None),
        P("space", None),
        P("space"),
        P(),
        P(("harm", "samp"), "space"),
    )
    return jax.shard_map(
        per_device,
        mesh=mesh,
        in_specs=placed,
        out_specs=P(("harm", "samp"), "space"),
        check_vma=False,
    )
```

time: 24.7 us -> 22.8 us (0.923)
  Pallas kernels: 23.9 us -> 22 us
    pallas_call x1, Pallas kernels: 23.9 us -> 22 us  [per_device(): pl.pallas_call(kernel, out_shape=pltpu.VMEM(source.shape, F32), in_specs=...]
where the time goes in v6:
time: 22.8 us; the launch traced here: 22.6 us
  Pallas kernels  22 us (96%)
  other arithmetic  0.62 us (3%)
    pallas_call x1, Pallas kernels, per_device(): pl.pallas_call(kernel, out_shape=pltpu.VMEM(source.shape, F32), in_specs=...  22 us
    sub x1, other arithmetic, per_device(): return total - source  0.62 us

profile of v6, /device:TPU:1, one launch (start us, length us, event | category | flops | bytes accessed | tf_op | source)
XLA Modules:
  0.0 22.6 jit_solution(4649698031015812826)
XLA Ops:
  0.0 0.0 copy-start
  0.0 22.0 %residual.1 = f32[2,2048]{1,0:T(2,128)S(1)} custom-call(bf16[2,2048]{1,0:T(2,128)(2,1)} %coef_hbm.1, bf16[16,4,128,384]{3,2,1,0:T(8,128)(2,1)} %curl_hbm.1, s32[4,16]{1,0:T(4,128)} %bitcast.1, s32[16]{0:T(128)} %reg_hbm.1, f32[3,4]{1,0:T(4,128)} %law_hbm.1, bf16[416,128]{1,0:T(8,128)(2,1)} %constant.2.clone.tab_hbm), custom_call_target="tpu_custom_call" | custom-call | tf_op jit(solution)/shard_map/residual/pallas_call | solution.py:298
  22.0 0.0 copy-done
  22.0 0.6 %sub.3 = f32[2,2048]{1,0:T(2,128)} subtract(f32[2,2048]{1,0:T(2,128)S(1)} %residual.1, f32[2,2048]{1,0:T(2,128)S(1)} %copy-done) | non-fusion elementwise | flops 4096 | bytes 49152 | tf_op jit(solution)/shard_map/sub | solution.py:328
Async XLA Ops:
  0.0 22.0 %copy-start = (f32[2,2048]{1,0:T(2,128)S(1)}, f32[2,2048]{1,0:T(2,128)}, u32[]{:S(2)}) copy-start(f32[2,2048]{1,0:T(2,128)} %param.12) | copy-start | bytes 49156

commit v7 on v6

--- a/solution.py
+++ b/solution.py
@@ -43,15 +43,17 @@
     main = np.zeros((LINKS, HALF, GROUP, LINKS, 2))
     for k in range(LINKS):
         main[k, :, :, k, :] = by_rank
-    main = main.reshape(WAVES, TILE)
-    halo = np.zeros((2, 2 * HALF, TILE), ml_dtypes.bfloat16)
-    for side in range(2):
-        halo[side, :, side * PARTS : (side + 1) * PARTS] = np.concatenate(two_pieces(transform))
+    main = np.concatenate(two_pieces(main.reshape(WAVES, TILE)), axis=1)
+    halo = np.zeros((2, HALF, 2, 2, PARTS), ml_dtypes.bfloat16)
+    for piece, part in enumerate(two_pieces(transform)):
+        for side in range(2):
+            halo[side, :, piece, side] = part
+    halo = np.pad(halo.reshape(2 * HALF, TILE), ((0, 0), (0, TILE)))
     back = (4.0 / SAMPLES) * by_rank.transpose(2, 1, 0).reshape(PARTS, HALF)
     back_high, back_low = two_pieces(back)
-    back_row = np.zeros((PARTS, TILE), ml_dtypes.bfloat16)
+    back_row = np.zeros((PARTS, 2 * TILE), ml_dtypes.bfloat16)
     back_row[:, : 3 * HALF] = np.concatenate([back_high, back_low, back_high], axis=1)
-    return np.concatenate([*two_pieces(main), halo.reshape(4 * HALF, TILE), back_row], axis=0)
+    return np.concatenate([main, halo, back_row], axis=0)
 
 
 def split(value):
@@ -62,7 +64,7 @@
 def kernel(
     coef_hbm, curl_hbm, pat_hbm, reg_hbm, law_hbm, tab_hbm, out_ref,
     coef, curl, pat, reg, law, tab, picks, got, firsts, low_got, high_got,
-    flow, flow_got, edge_flow, low_flow, high_flow, local_sem, send_sem, recv_sem, ready,
+    flow, flow_got, edge_flow, low_flow, high_flow, local_sem, send_sem, recv_sem, ready, curl_t,
 ):
     harm, space, samp = lax.axis_index("harm"), lax.axis_index("space"), lax.axis_index("samp")
     rank = harm * 4 + samp
@@ -87,17 +89,25 @@
         pltpu.make_async_copy(tab_hbm, tab, local_sem.at[4]),
         pltpu.make_async_copy(curl_hbm.at[pl.ds(OWN * samp, OWN)], curl, local_sem.at[5]),
     ]
+    barrier = pltpu.get_barrier_semaphore()
+
+    @pl.when(is_hub)
+    def _():
+        def greet(group, other):
+            pl.semaphore_signal(barrier, inc=1, device_id=at(group, other), device_id_type=MESH)
+
+        for other in hubs:
+            greet(space, other)
+            greet(before, other)
+        for other in reversed(plain):
+            greet(space, other)
+            greet(before, other)
+        greet(before, home)
+        for load in loads[4:]:
+            load.start()
+
     for load in loads[:4]:
         load.start()
-    barrier = pltpu.get_barrier_semaphore()
-
-    @pl.when(is_hub)
-    def _():
-        for group, others in ((space, hubs), (before, [*hubs, home]), (space, plain), (before, plain)):
-            for other in others:
-                pl.semaphore_signal(barrier, inc=1, device_id=at(group, other), device_id_type=MESH)
-        for load in loads[4:]:
-            load.start()
 
     loads[0].wait()
     loads[1].wait()
@@ -178,6 +188,8 @@
     def _():
         firsts[rank] = coef[:, 0:TILE]
         got[rank] = picks[samp]
+        for v in range(OWN):
+            curl_t[v] = curl[v].reshape(LINKS * TILE, COMP).T
         gathered = firsts.at[pl.ds(0, GROUP - 1)]
         remote(gathered, gathered, 0, space, hubs[0]).wait_recv()
         pl.semaphore_wait(ready, 1)
@@ -185,28 +197,32 @@
         handed.start()
         picked = got.at[pl.ds(0, GROUP - 1)]
         remote(picked, picked, 3, space, hubs[0]).wait_recv()
-        waves = []
-        for v in range(OWN):
-            window = got[:, v].reshape(GROUP * EDGE, TILE)
-            wave = jnp.dot(tab[0 : 2 * WAVES, :], window, preferred_element_type=F32)
-            waves.append(wave[:WAVES] + wave[WAVES:])
+        windows = jnp.concatenate(
+            [got[:, v].reshape(GROUP * EDGE, TILE) for v in range(OWN)], axis=1
+        )
+        waves = jnp.dot(
+            tab[0:WAVES, :],
+            jnp.concatenate([windows, windows], axis=0),
+            preferred_element_type=F32,
+        )
         remote(low_got, low_got, 1, space, hubs[0]).wait_recv()
         handed.wait_recv()
         halo = [
             ref[...].astype(F32).reshape(PARTS, TILE).astype(BF16) for ref in (low_got, high_got)
         ]
         halo = jnp.dot(
-            tab[2 * WAVES : 2 * WAVES + 4 * HALF, 0 : 2 * PARTS],
-            jnp.concatenate(halo, axis=0),
+            tab[WAVES : WAVES + 2 * HALF, 0:TILE],
+            jnp.concatenate([*halo, *halo], axis=0),
             preferred_element_type=F32,
         )
-        halo = [halo[2 * i * HALF :][:HALF] + halo[(2 * i + 1) * HALF :][:HALF] for i in range(2)]
-        back = tab[2 * WAVES + 4 * HALF : 2 * WAVES + 4 * HALF + PARTS, 0 : 3 * HALF]
+        halo = [halo[:HALF], halo[HALF:]]
+        back = tab[WAVES + 2 * HALF : WAVES + 2 * HALF + PARTS, 0 : 3 * HALF]
+        contribs = []
         edges = [jnp.zeros((PARTS, TILE), F32), jnp.zeros((PARTS, TILE), F32)]
         for v in range(OWN):
             wave = []
             for k in range(LINKS):
-                piece = waves[v][k * HALF : (k + 1) * HALF]
+                piece = waves[k * HALF : (k + 1) * HALF, v * TILE : (v + 1) * TILE]
                 for i, spot in enumerate((0, TILES + 1)):
                     piece = piece + jnp.where(links[v][:, k : k + 1] == spot, halo[i], 0.0)
                 wave.append(piece)
@@ -225,15 +241,12 @@
             harmonic = jnp.dot(
                 back, jnp.concatenate([high, high, low], axis=0), preferred_element_type=F32
             )
-            contrib = lax.dot_general(
-                harmonic.astype(BF16), blocks, (((1,), (1,)), ((), ())), preferred_element_type=F32
+            contrib = jnp.dot(
+                harmonic.astype(BF16), curl_t[v], preferred_element_type=F32
             )
+            contribs.append(contrib)
             for k in range(LINKS):
                 tile = contrib[:, k * TILE : (k + 1) * TILE]
-                for p in range(2):
-                    flow[pl.ds(v * EDGE + 2 * k + p, GROUP, stride=ROWS), :] = tile[
-                        p * GROUP : (p + 1) * GROUP
-                    ]
                 for i, spot in enumerate((0, TILES + 1)):
                     edges[i] = edges[i] + jnp.where(links[v][:, k : k + 1] == spot, tile, 0.0)
         for i in range(2):
@@ -243,14 +256,21 @@
         to_after = [remote(edge_flow.at[1, o], low_flow.at[samp], 4, after, o) for o in launched]
         to_before = [remote(edge_flow.at[0, o], high_flow.at[samp], 5, before, o) for o in launched]
         to_group = [remote(block(flow, o), block(flow_got, samp), 6, space, o) for o in launched]
-        for other, *copies in zip(launched, to_after, to_group, to_before):
-            copies[0].start()
+        for copy in to_after:
+            copy.start()
+        for v in range(OWN):
+            for k in range(LINKS):
+                for p in range(2):
+                    flow[pl.ds(v * EDGE + 2 * k + p, GROUP, stride=ROWS), :] = contribs[v][
+                        p * GROUP : (p + 1) * GROUP, k * TILE : (k + 1) * TILE
+                    ]
+        for other, *copies in zip(launched, to_group, to_before):
 
             @pl.when(rank != other)
             def _():
-                copies[1].start()
-
-            copies[2].start()
+                copies[0].start()
+
+            copies[1].start()
         mine = pl.ds(pl.multiple_of(samp * ROWS, ROWS), ROWS)
         flow_got[mine, :] = flow[pl.ds(pl.multiple_of(rank * ROWS, ROWS), ROWS), :]
         others = pl.ds(0, (HUBS - 1) * ROWS)
@@ -321,6 +341,7 @@
             pltpu.SemaphoreType.DMA((7,)),
             pltpu.SemaphoreType.DMA((7,)),
             pltpu.SemaphoreType.REGULAR,
+            pltpu.VMEM((OWN, COMP, LINKS * TILE), BF16),
         ],
         compiler_params=pltpu.CompilerParams(collective_id=0, has_side_effects=True),
         name="residual",

time: 22.8 us -> 22.4 us (0.982)
  Pallas kernels: 22 us -> 21.7 us
    pallas_call x1, Pallas kernels: 22 us -> 21.7 us  [per_device(): pl.pallas_call(kernel, out_shape=pltpu.VMEM(source.shape, F32), in_specs=...]
where the time goes in v7:
time: 22.4 us; the launch traced here: 22.3 us
  Pallas kernels  21.7 us (97%)
  other arithmetic  0.62 us (3%)
    pallas_call x1, Pallas kernels, per_device(): pl.pallas_call(kernel, out_shape=pltpu.VMEM(source.shape, F32), in_specs=...  21.7 us
    sub x1, other arithmetic, per_device(): return total - source  0.62 us

profile of v7, /device:TPU:1, one launch (start us, length us, event | category | flops | bytes accessed | tf_op | source)
XLA Modules:
  0.0 22.3 jit_solution(6474241182812097786)
XLA Ops:
  0.0 0.0 copy-start
  0.0 21.7 %residual.1 = f32[2,2048]{1,0:T(2,128)S(1)} custom-call(bf16[2,2048]{1,0:T(2,128)(2,1)} %coef_hbm.1, bf16[16,4,128,384]{3,2,1,0:T(8,128)(2,1)} %curl_hbm.1, s32[4,16]{1,0:T(4,128)} %bitcast.1, s32[16]{0:T(128)} %reg_hbm.1, f32[3,4]{1,0:T(4,128)} %law_hbm.1, bf16[224,256]{1,0:T(8,128)(2,1)} %constant.2.clone.tab_hbm), custom_call_target="tpu_custom_call" | custom-call | tf_op jit(solution)/shard_map/residual/pallas_call | solution.py:318
  21.7 0.0 copy-done
  21.7 0.6 %sub.3 = f32[2,2048]{1,0:T(2,128)} subtract(f32[2,2048]{1,0:T(2,128)S(1)} %residual.1, f32[2,2048]{1,0:T(2,128)S(1)} %copy-done) | non-fusion elementwise | flops 4096 | bytes 49152 | tf_op jit(solution)/shard_map/sub | solution.py:349
Async XLA Ops:
  0.0 21.7 %copy-start = (f32[2,2048]{1,0:T(2,128)S(1)}, f32[2,2048]{1,0:T(2,128)}, u32[]{:S(2)}) copy-start(f32[2,2048]{1,0:T(2,128)} %param.12) | copy-start | bytes 49156

commit v8 on v7

--- a/solution.py
+++ b/solution.py
@@ -217,8 +217,8 @@
         )
         halo = [halo[:HALF], halo[HALF:]]
         back = tab[WAVES + 2 * HALF : WAVES + 2 * HALF + PARTS, 0 : 3 * HALF]
-        contribs = []
         edges = [jnp.zeros((PARTS, TILE), F32), jnp.zeros((PARTS, TILE), F32)]
+        densities = []
         for v in range(OWN):
             wave = []
             for k in range(LINKS):
@@ -226,27 +226,29 @@
                 for i, spot in enumerate((0, TILES + 1)):
                     piece = piece + jnp.where(links[v][:, k : k + 1] == spot, halo[i], 0.0)
                 wave.append(piece)
-            blocks = curl[v].reshape(LINKS * TILE, COMP)
-            density = jnp.dot(
-                jnp.concatenate(split(jnp.concatenate(wave, axis=1)), axis=0),
-                blocks,
-                preferred_element_type=F32,
+            densities.append(
+                jnp.dot(
+                    jnp.concatenate(split(jnp.concatenate(wave, axis=1)), axis=0),
+                    curl[v].reshape(LINKS * TILE, COMP),
+                    preferred_element_type=F32,
+                )
             )
-            density = density[:HALF] + density[HALF:]
+        fields = []
+        for v in range(OWN):
+            density = densities[v][:HALF] + densities[v][HALF:]
             comps = [density[:, c * TILE : (c + 1) * TILE] for c in range(3)]
             square = comps[0] * comps[0] + comps[1] * comps[1] + comps[2] * comps[2]
             base, knee, rise = laws[v]
             reluct = base + rise * square / (square + knee)
             high, low = split(jnp.concatenate([reluct * c for c in comps], axis=1))
-            harmonic = jnp.dot(
-                back, jnp.concatenate([high, high, low], axis=0), preferred_element_type=F32
-            )
-            contrib = jnp.dot(
-                harmonic.astype(BF16), curl_t[v], preferred_element_type=F32
-            )
-            contribs.append(contrib)
+            fields.append(jnp.concatenate([high, high, low], axis=0))
+        harmonics = [jnp.dot(back, f, preferred_element_type=F32).astype(BF16) for f in fields]
+        contribs = [
+            jnp.dot(harmonics[v], curl_t[v], preferred_element_type=F32) for v in range(OWN)
+        ]
+        for v in range(OWN):
             for k in range(LINKS):
-                tile = contrib[:, k * TILE : (k + 1) * TILE]
+                tile = contribs[v][:, k * TILE : (k + 1) * TILE]
                 for i, spot in enumerate((0, TILES + 1)):
                     edges[i] = edges[i] + jnp.where(links[v][:, k : k + 1] == spot, tile, 0.0)
         for i in range(2):

time: 22.4 us -> 21.6 us (0.964)
  Pallas kernels: 21.7 us -> 20.8 us
    pallas_call x1, Pallas kernels: 21.7 us -> 20.8 us  [per_device(): pl.pallas_call(kernel, out_shape=pltpu.VMEM(source.shape, F32), in_specs=...]
where the time goes in v8:
time: 21.6 us; the launch traced here: 21.5 us
  Pallas kernels  20.8 us (96%)
  other arithmetic  0.62 us (3%)
    pallas_call x1, Pallas kernels, per_device(): pl.pallas_call(kernel, out_shape=pltpu.VMEM(source.shape, F32), in_specs=...  20.8 us
    sub x1, other arithmetic, per_device(): return total - source  0.62 us

profile of v8, /device:TPU:1, one launch (start us, length us, event | category | flops | bytes accessed | tf_op | source)
XLA Modules:
  0.0 21.5 jit_solution(11567847037784789219)
XLA Ops:
  0.0 0.0 copy-start
  0.0 20.8 %residual.1 = f32[2,2048]{1,0:T(2,128)S(1)} custom-call(bf16[2,2048]{1,0:T(2,128)(2,1)} %coef_hbm.1, bf16[16,4,128,384]{3,2,1,0:T(8,128)(2,1)} %curl_hbm.1, s32[4,16]{1,0:T(4,128)} %bitcast.1, s32[16]{0:T(128)} %reg_hbm.1, f32[3,4]{1,0:T(4,128)} %law_hbm.1, bf16[224,256]{1,0:T(8,128)(2,1)} %constant.2.clone.tab_hbm), custom_call_target="tpu_custom_call" | custom-call | tf_op jit(solution)/shard_map/residual/pallas_call | solution.py:320
  20.8 0.0 copy-done
  20.8 0.6 %sub.3 = f32[2,2048]{1,0:T(2,128)} subtract(f32[2,2048]{1,0:T(2,128)S(1)} %residual.1, f32[2,2048]{1,0:T(2,128)S(1)} %copy-done) | non-fusion elementwise | flops 4096 | bytes 49152 | tf_op jit(solution)/shard_map/sub | solution.py:351
Async XLA Ops:
  0.0 20.8 %copy-start = (f32[2,2048]{1,0:T(2,128)S(1)}, f32[2,2048]{1,0:T(2,128)}, u32[]{:S(2)}) copy-start(f32[2,2048]{1,0:T(2,128)} %param.12) | copy-start | bytes 49156

commit v9 on v8

--- a/solution.py
+++ b/solution.py
@@ -14,7 +14,6 @@
 PARTS = 32
 GROUP = 16
 HUBS = 4
-HUB = 4
 OWN = 4
 SPACE = 16
 TILES = 16
@@ -68,7 +67,8 @@
 ):
     harm, space, samp = lax.axis_index("harm"), lax.axis_index("space"), lax.axis_index("samp")
     rank = harm * 4 + samp
-    is_hub = harm == 1
+    is_hub = jnp.logical_or(jnp.logical_and(harm == 1, samp < 3), rank == 0)
+    spoke = jnp.where(rank == 0, 3, samp)
     after, before = lax.rem(space + 1, SPACE), lax.rem(space + SPACE - 1, SPACE)
 
     def at(group, other):
@@ -76,10 +76,14 @@
             return (other // 4, group, other % 4)
         return (other // 4, group, lax.rem(other, 4))
 
-    home = HUB + samp
-    hubs = [HUB + lax.rem(samp + d, HUBS) for d in range(1, HUBS)]
+    def hub_rank(u):
+        return jnp.where(u == 3, 0, 4 + u)
+
+    home = hub_rank(spoke)
+    others_spokes = [lax.rem(spoke + d, HUBS) for d in range(1, HUBS)]
+    hubs = [hub_rank(u) for u in others_spokes]
     launched = [(z // 4 * 2 + c) * 4 + z % 4 for z in range(8) for c in (1, 0)]
-    plain = [other for other in launched if other // 4 != 1]
+    plain = [other for other in launched if other not in (0, 4, 5, 6)]
 
     loads = [
         pltpu.make_async_copy(coef_hbm, coef, local_sem.at[0]),
@@ -87,7 +91,7 @@
         pltpu.make_async_copy(reg_hbm, reg, local_sem.at[2]),
         pltpu.make_async_copy(law_hbm, law, local_sem.at[3]),
         pltpu.make_async_copy(tab_hbm, tab, local_sem.at[4]),
-        pltpu.make_async_copy(curl_hbm.at[pl.ds(OWN * samp, OWN)], curl, local_sem.at[5]),
+        pltpu.make_async_copy(curl_hbm.at[pl.ds(OWN * spoke, OWN)], curl, local_sem.at[5]),
     ]
     barrier = pltpu.get_barrier_semaphore()
 
@@ -132,7 +136,7 @@
     loads[3].wait()
     links, laws = [], []
     for v in range(OWN):
-        element = OWN * samp + v
+        element = OWN * spoke + v
         own_row = lax.broadcasted_iota(jnp.int32, (TILES, LINKS), 0) == element
         links.append(jnp.sum(jnp.where(own_row, pattern, 0), axis=0, keepdims=True))
         region = reg[...].reshape(1, TILES)
@@ -162,9 +166,11 @@
     first, last = coef.at[:, pl.ds(0, TILE)], coef.at[:, pl.ds((TILES - 1) * TILE, TILE)]
     sent_first = [remote(first, firsts.at[rank], 0, space, other) for other in hubs]
     sent_last = [remote(last, low_got.at[rank], 1, after, other) for other in [home, *hubs]]
-    sent_picks = [remote(picks.at[other - HUB], got.at[rank], 3, space, other) for other in hubs]
+    sent_picks = [
+        remote(picks.at[u], got.at[rank], 3, space, hub_rank(u)) for u in others_spokes
+    ]
     home_first = remote(first, firsts.at[rank], 0, space, home)
-    home_picks = remote(picks.at[samp], got.at[rank], 3, space, home)
+    home_picks = remote(picks.at[spoke], got.at[rank], 3, space, home)
 
     @pl.when(jnp.logical_not(is_hub))
     def _():
@@ -187,7 +193,7 @@
     @pl.when(is_hub)
     def _():
         firsts[rank] = coef[:, 0:TILE]
-        got[rank] = picks[samp]
+        got[rank] = picks[spoke]
         for v in range(OWN):
             curl_t[v] = curl[v].reshape(LINKS * TILE, COMP).T
         gathered = firsts.at[pl.ds(0, GROUP - 1)]
@@ -255,9 +261,9 @@
             for p in range(2):
                 edge_flow[i, :, p, :] = edges[i][p * GROUP : (p + 1) * GROUP]
 
-        to_after = [remote(edge_flow.at[1, o], low_flow.at[samp], 4, after, o) for o in launched]
-        to_before = [remote(edge_flow.at[0, o], high_flow.at[samp], 5, before, o) for o in launched]
-        to_group = [remote(block(flow, o), block(flow_got, samp), 6, space, o) for o in launched]
+        to_after = [remote(edge_flow.at[1, o], low_flow.at[spoke], 4, after, o) for o in launched]
+        to_before = [remote(edge_flow.at[0, o], high_flow.at[spoke], 5, before, o) for o in launched]
+        to_group = [remote(block(flow, o), block(flow_got, spoke), 6, space, o) for o in launched]
         for copy in to_after:
             copy.start()
         for v in range(OWN):
@@ -273,7 +279,7 @@
                 copies[0].start()
 
             copies[1].start()
-        mine = pl.ds(pl.multiple_of(samp * ROWS, ROWS), ROWS)
+        mine = pl.ds(pl.multiple_of(spoke * ROWS, ROWS), ROWS)
         flow_got[mine, :] = flow[pl.ds(pl.multiple_of(rank * ROWS, ROWS), ROWS), :]
         others = pl.ds(0, (HUBS - 1) * ROWS)
         remote(flow_got.at[others], flow_got.at[others], 6, space, hubs[0]).wait_recv()
@@ -282,21 +288,11 @@
     def _():
         remote(flow_got, flow_got, 6, space, home).wait_recv()
 
-    remote(low_flow, low_flow, 4, after, home).wait_recv()
-    remote(high_flow, high_flow, 5, after, home).wait_recv()
     owned = jnp.dot(
         spread, jnp.concatenate(split(flow_got[...]), axis=0), preferred_element_type=F32
     )
-    low_sum, high_sum = low_flow[0], high_flow[0]
-    for u in range(1, HUBS):
-        low_sum, high_sum = low_sum + low_flow[u], high_sum + high_flow[u]
-    for w in range(TILES):
-        piece = owned[2 * w : 2 * w + 2]
-        if w == 0:
-            piece = piece + low_sum
-        if w == TILES - 1:
-            piece = piece + high_sum
-        out_ref[:, w * TILE : (w + 1) * TILE] = piece
+    for w in range(1, TILES - 1):
+        out_ref[:, w * TILE : (w + 1) * TILE] = owned[2 * w : 2 * w + 2]
     for copy in sent_first + sent_last + sent_picks:
         copy.wait_send()
 
@@ -312,6 +308,11 @@
         remote(edge_flow.at[1], edge_flow.at[1], 4, after, home).wait_send()
         remote(edge_flow.at[0], edge_flow.at[0], 5, after, home).wait_send()
         remote(flow.at[others], flow.at[others], 6, after, home).wait_send()
+
+    for w, edge, i in ((TILES - 1, high_flow, 5), (0, low_flow, 4)):
+        remote(edge, edge, i, after, home).wait_recv()
+        edge_sum = (edge[0] + edge[1]) + (edge[2] + edge[3])
+        out_ref[:, w * TILE : (w + 1) * TILE] = owned[2 * w : 2 * w + 2] + edge_sum
 
 
 def per_device(coeffs, curl_tiles, pattern, region_ids, material_law, source):

time: 21.6 us -> 21.3 us (0.986)
  Pallas kernels: 20.8 us -> 20.5 us
    pallas_call x1, Pallas kernels: 20.8 us -> 20.5 us  [per_device(): pl.pallas_call(kernel, out_shape=pltpu.VMEM(source.shape, F32), in_specs=...]
where the time goes in v9:
time: 21.3 us; the launch traced here: 21.2 us
  Pallas kernels  20.5 us (96%)
  other arithmetic  0.62 us (3%)
    pallas_call x1, Pallas kernels, per_device(): pl.pallas_call(kernel, out_shape=pltpu.VMEM(source.shape, F32), in_specs=...  20.5 us
    sub x1, other arithmetic, per_device(): return total - source  0.62 us

profile of v9, /device:TPU:1, one launch (start us, length us, event | category | flops | bytes accessed | tf_op | source)
XLA Modules:
  0.0 21.2 jit_solution(14040010381423478919)
XLA Ops:
  0.0 0.0 copy-start
  0.0 20.5 %residual.1 = f32[2,2048]{1,0:T(2,128)S(1)} custom-call(bf16[2,2048]{1,0:T(2,128)(2,1)} %coef_hbm.1, bf16[16,4,128,384]{3,2,1,0:T(8,128)(2,1)} %curl_hbm.1, s32[4,16]{1,0:T(4,128)} %bitcast.1, s32[16]{0:T(128)} %reg_hbm.1, f32[3,4]{1,0:T(4,128)} %law_hbm.1, bf16[224,256]{1,0:T(8,128)(2,1)} %constant.2.clone.tab_hbm), custom_call_target="tpu_custom_call" | custom-call | tf_op jit(solution)/shard_map/residual/pallas_call | solution.py:321
  20.5 0.0 copy-done
  20.6 0.6 %sub.3 = f32[2,2048]{1,0:T(2,128)} subtract(f32[2,2048]{1,0:T(2,128)S(1)} %residual.1, f32[2,2048]{1,0:T(2,128)S(1)} %copy-done) | non-fusion elementwise | flops 4096 | bytes 49152 | tf_op jit(solution)/shard_map/sub | solution.py:352
Async XLA Ops:
  0.0 20.5 %copy-start = (f32[2,2048]{1,0:T(2,128)S(1)}, f32[2,2048]{1,0:T(2,128)}, u32[]{:S(2)}) copy-start(f32[2,2048]{1,0:T(2,128)} %param.12) | copy-start | bytes 49156

commit v10 on v9

--- a/solution.py
+++ b/solution.py
@@ -103,10 +103,10 @@
         for other in hubs:
             greet(space, other)
             greet(before, other)
+        greet(before, home)
         for other in reversed(plain):
             greet(space, other)
             greet(before, other)
-        greet(before, home)
         for load in loads[4:]:
             load.start()
 

time: 21.3 us -> 21.3 us (level)
  no operation moved by 1% of the time
where the time goes in v10:
time: 21.3 us; the launch traced here: 21.2 us
  Pallas kernels  20.5 us (96%)
  other arithmetic  0.62 us (3%)
    pallas_call x1, Pallas kernels, per_device(): pl.pallas_call(kernel, out_shape=pltpu.VMEM(source.shape, F32), in_specs=...  20.5 us
    sub x1, other arithmetic, per_device(): return total - source  0.62 us

profile of v10, /device:TPU:1, one launch (start us, length us, event | category | flops | bytes accessed | tf_op | source)
XLA Modules:
  0.0 21.2 jit_solution(13732102122723404665)
XLA Ops:
  0.0 0.0 copy-start
  0.0 20.5 %residual.1 = f32[2,2048]{1,0:T(2,128)S(1)} custom-call(bf16[2,2048]{1,0:T(2,128)(2,1)} %coef_hbm.1, bf16[16,4,128,384]{3,2,1,0:T(8,128)(2,1)} %curl_hbm.1, s32[4,16]{1,0:T(4,128)} %bitcast.1, s32[16]{0:T(128)} %reg_hbm.1, f32[3,4]{1,0:T(4,128)} %law_hbm.1, bf16[224,256]{1,0:T(8,128)(2,1)} %constant.2.clone.tab_hbm), custom_call_target="tpu_custom_call" | custom-call | tf_op jit(solution)/shard_map/residual/pallas_call | solution.py:321
  20.5 0.0 copy-done
  20.6 0.6 %sub.3 = f32[2,2048]{1,0:T(2,128)} subtract(f32[2,2048]{1,0:T(2,128)S(1)} %residual.1, f32[2,2048]{1,0:T(2,128)S(1)} %copy-done) | non-fusion elementwise | flops 4096 | bytes 49152 | tf_op jit(solution)/shard_map/sub | solution.py:352
Async XLA Ops:
  0.0 20.5 %copy-start = (f32[2,2048]{1,0:T(2,128)S(1)}, f32[2,2048]{1,0:T(2,128)}, u32[]{:S(2)}) copy-start(f32[2,2048]{1,0:T(2,128)} %param.12) | copy-start | bytes 49156

commit v11 on v9

--- a/solution.py
+++ b/solution.py
@@ -161,7 +161,9 @@
 
     @pl.when(is_hub)
     def _():
-        pl.semaphore_signal(ready, inc=1, device_id=at(after, rank), device_id_type=MESH)
+        pl.semaphore_signal(
+            ready, inc=1, device_id=at(after, jnp.where(rank == 0, 4, rank)), device_id_type=MESH
+        )
 
     first, last = coef.at[:, pl.ds(0, TILE)], coef.at[:, pl.ds((TILES - 1) * TILE, TILE)]
     sent_first = [remote(first, firsts.at[rank], 0, space, other) for other in hubs]
@@ -198,9 +200,17 @@
             curl_t[v] = curl[v].reshape(LINKS * TILE, COMP).T
         gathered = firsts.at[pl.ds(0, GROUP - 1)]
         remote(gathered, gathered, 0, space, hubs[0]).wait_recv()
-        pl.semaphore_wait(ready, 1)
         handed = remote(firsts, high_got, 2, before, rank)
-        handed.start()
+
+        @pl.when(rank != 0)
+        def _():
+            pl.semaphore_wait(ready, jnp.where(rank == 4, 2, 1))
+            handed.start()
+
+        @pl.when(rank == 4)
+        def _():
+            remote(firsts, high_got, 2, before, 0).start()
+
         picked = got.at[pl.ds(0, GROUP - 1)]
         remote(picked, picked, 3, space, hubs[0]).wait_recv()
         windows = jnp.concatenate(
@@ -212,10 +222,9 @@
             preferred_element_type=F32,
         )
         remote(low_got, low_got, 1, space, hubs[0]).wait_recv()
+        halo = [low_got[...].astype(F32).reshape(PARTS, TILE).astype(BF16)]
         handed.wait_recv()
-        halo = [
-            ref[...].astype(F32).reshape(PARTS, TILE).astype(BF16) for ref in (low_got, high_got)
-        ]
+        halo.append(high_got[...].astype(F32).reshape(PARTS, TILE).astype(BF16))
         halo = jnp.dot(
             tab[WAVES : WAVES + 2 * HALF, 0:TILE],
             jnp.concatenate([*halo, *halo], axis=0),
@@ -304,7 +313,15 @@
     @pl.when(is_hub)
     def _():
         others = pl.ds(0, (GROUP - 1) * ROWS)
-        remote(firsts, high_got, 2, before, rank).wait_send()
+
+        @pl.when(rank != 0)
+        def _():
+            remote(firsts, high_got, 2, before, rank).wait_send()
+
+        @pl.when(rank == 4)
+        def _():
+            remote(firsts, high_got, 2, before, 0).wait_send()
+
         remote(edge_flow.at[1], edge_flow.at[1], 4, after, home).wait_send()
         remote(edge_flow.at[0], edge_flow.at[0], 5, after, home).wait_send()
         remote(flow.at[others], flow.at[others], 6, after, home).wait_send()

time: 21.3 us -> 21.3 us (level)
  no operation moved by 1% of the time
where the time goes in v11:
time: 21.3 us; the launch traced here: 21.2 us
  Pallas kernels  20.5 us (96%)
  other arithmetic  0.62 us (3%)
    pallas_call x1, Pallas kernels, per_device(): pl.pallas_call(kernel, out_shape=pltpu.VMEM(source.shape, F32), in_specs=...  20.5 us
    sub x1, other arithmetic, per_device(): return total - source  0.62 us

profile of v11, /device:TPU:1, one launch (start us, length us, event | category | flops | bytes accessed | tf_op | source)
XLA Modules:
  0.0 21.2 jit_solution(8045431880077736783)
XLA Ops:
  0.0 0.0 copy-start
  0.0 20.5 %residual.1 = f32[2,2048]{1,0:T(2,128)S(1)} custom-call(bf16[2,2048]{1,0:T(2,128)(2,1)} %coef_hbm.1, bf16[16,4,128,384]{3,2,1,0:T(8,128)(2,1)} %curl_hbm.1, s32[4,16]{1,0:T(4,128)} %bitcast.1, s32[16]{0:T(128)} %reg_hbm.1, f32[3,4]{1,0:T(4,128)} %law_hbm.1, bf16[224,256]{1,0:T(8,128)(2,1)} %constant.2.clone.tab_hbm), custom_call_target="tpu_custom_call" | custom-call | tf_op jit(solution)/shard_map/residual/pallas_call | solution.py:338
  20.5 0.0 copy-done
  20.5 0.6 %sub.3 = f32[2,2048]{1,0:T(2,128)} subtract(f32[2,2048]{1,0:T(2,128)S(1)} %residual.1, f32[2,2048]{1,0:T(2,128)S(1)} %copy-done) | non-fusion elementwise | flops 4096 | bytes 49152 | tf_op jit(solution)/shard_map/sub | solution.py:369
Async XLA Ops:
  0.0 20.5 %copy-start = (f32[2,2048]{1,0:T(2,128)S(1)}, f32[2,2048]{1,0:T(2,128)}, u32[]{:S(2)}) copy-start(f32[2,2048]{1,0:T(2,128)} %param.12) | copy-start | bytes 49156
